TPU v7x, 512 devices: a whole 4x8x8 slice. The times are simulated.
512 devices in a mesh: ctx: 128 (over y, z, core), head: 4 (over x).
Axes of the slice: x: 4, y: 8, z: 8, core: 2. Of those that a mesh axis runs over, the one named last changes fastest.
Arguments:
- queries: bfloat16 [16384, 64, 576], P('ctx', 'head'), may hold values from -18 to 18
- latent: bfloat16 [16384, 576], P('ctx'), may hold values from -4 to 4
- out_grad: bfloat16 [16384, 64, 512], P('ctx', 'head'), may hold values from -4 to 4
- doc_blocks: int32 [64], replicated, may hold values from 1 to 4, as said below
Outputs:
- latent_grad: float32 [16384, 576], P('ctx')
Inputs may be any that keep to these rules, and one draw needn't show every extreme that they name: `doc_blocks`: they sum to 128; the longest document has exactly 4 blocks.
All inputs are finite; a program needn't handle non-finite values.
Results may differ from a plain program's by a relative error of at most 0.007.
Values may be sent and summed in bfloat16 or wider, within the bound.
No kernel may reach another device: no remote copies, remote signals or barrier semaphores. Data moves between devices by JAX's collectives and lax.ppermute only.
A program may use at most 64 MiB of HBM per device.

v0:
```python
import jax
import jax.numpy as jnp
from jax import lax
from jax.sharding import PartitionSpec as P

BLOCK = 128
BACK = 3


softmax_scale = 192.0 ** (-0.5)


def passed_along(x, axis, by):
    peers = lax.axis_size(axis)
    pairs = [(i, i + by) for i in range(peers) if 0 <= i + by < peers]
    return lax.ppermute(x, axis, pairs)


def doc_index(position, starts):
    return jnp.sum((position[:, None] >= starts[None, :]).astype(jnp.int32), axis=1)


def window_grads(query_rows, grad_rows, window, visible):
    lat_width = grad_rows.shape[-1]
    scores = (
        jnp.einsum("thc,uc->htu", query_rows, window, preferred_element_type=jnp.float32)
        * softmax_scale
    )
    scores = jnp.where(visible[None], scores, -jnp.inf)
    row_max = jnp.max(scores, axis=-1, keepdims=True)
    raised = jnp.exp(scores - row_max)
    attn_probs = raised / jnp.sum(raised, axis=-1, keepdims=True)
    probs_low = attn_probs.astype(jnp.bfloat16)
    grad_probs = jnp.einsum(
        "thc,uc->htu", grad_rows, window[:, :lat_width], preferred_element_type=jnp.float32
    )
    row_dot = jnp.sum(attn_probs * grad_probs, axis=-1, keepdims=True)
    grad_scores = (attn_probs * (grad_probs - row_dot) * softmax_scale).astype(jnp.bfloat16)
    value_part = jnp.einsum("htu,thc->uc", probs_low, grad_rows, preferred_element_type=jnp.float32)
    key_part = jnp.einsum(
        "htu,thc->uc", grad_scores, query_rows, preferred_element_type=jnp.float32
    )
    return jnp.concatenate([key_part[:, :lat_width] + value_part, key_part[:, lat_width:]], axis=1)


def send_direct_full(blocks):
    summed = blocks[BACK]
    for offset in range(1, BACK + 1):
        summed = summed + passed_along(blocks[BACK - offset], "ctx", -offset)
    return summed


def shards(queries, latent, out_grad, doc_blocks):
    tok_rows, key_width = latent.shape
    shard_index = lax.axis_index("ctx")
    pieces = [passed_along(latent, "ctx", offset) for offset in range(BACK, 0, -1)]
    window = jnp.concatenate(pieces + [latent], axis=0)
    starts = (jnp.cumsum(doc_blocks) - doc_blocks) * BLOCK
    first_row = shard_index * tok_rows
    query_pos = first_row + jnp.arange(tok_rows, dtype=jnp.int32)
    key_pos = first_row - BACK * tok_rows + jnp.arange((BACK + 1) * tok_rows, dtype=jnp.int32)
    same_doc = doc_index(query_pos, starts)[:, None] == doc_index(key_pos, starts)[None, :]
    visible = same_doc & (key_pos[None, :] <= query_pos[:, None])
    window_grad = window_grads(queries, out_grad, window, visible)
    blocks = window_grad.reshape(BACK + 1, tok_rows, key_width)
    summed = send_direct_full(blocks)
    result = lax.psum(summed, "head")
    return result


def solution(mesh):
    return jax.shard_map(
        shards,
        mesh=mesh,
        in_specs=(P("ctx", "head", None), P("ctx", None), P("ctx", "head", None), P()),
        out_specs=P("ctx", None),
        check_vma=False,
    )
```

profile of v0, /device:TPU:8, one launch (start us, length us, event | category | flops | bytes accessed | tf_op | source)
XLA Modules:
  0.0 134.2 jit_solution(10234687396069280848)
XLA Ops:
  6.5 0.0 copy-start
  6.5 0.0 copy-start.2
  6.5 0.0 all-reduce.2.cloned.1.call-start
  6.5 4.0 %collective-permute-start = (bf16[128,576]{0,1:T(8,128)(2,1)}, bf16[128,576]{0,1:T(8,128)(2,1)S(1)}, u32[]{:S(2)}, u32[]{:S(2)}) collective-permute-start(bf16[128,576]{0,1:T(8,128)(2,1)} %param.5), channel_id=1, source_target_pairs={{0,12},{4,16},{8,20},{12,24},{16,28},{20,32},{24,36},{28,40},{32,4... | collective-permute-start | bytes 442376 | tf_op jit(solution)/shard_map/ppermute | solution.py:16
  10.5 4.3 %collective-permute-start.1 = (bf16[128,576]{0,1:T(8,128)(2,1)}, bf16[128,576]{0,1:T(8,128)(2,1)S(1)}, u32[]{:S(2)}, u32[]{:S(2)}) collective-permute-start(bf16[128,576]{0,1:T(8,128)(2,1)} %param.5), channel_id=1, source_target_pairs={{0,8},{4,12},{8,16},{12,20},{16,24},{20,28},{24,32},{28,36},{32,40... | collective-permute-start | bytes 442376 | tf_op jit(solution)/shard_map/ppermute | solution.py:16
  14.8 4.1 %collective-permute-start.2 = (bf16[128,576]{0,1:T(8,128)(2,1)}, bf16[128,576]{0,1:T(8,128)(2,1)S(1)}, u32[]{:S(2)}, u32[]{:S(2)}) collective-permute-start(bf16[128,576]{0,1:T(8,128)(2,1)} %param.5), channel_id=1, source_target_pairs={{0,4},{4,8},{8,12},{12,16},{16,20},{20,24},{24,28},{28,32},{32,36}... | collective-permute-start | bytes 442376 | tf_op jit(solution)/shard_map/ppermute | solution.py:16
  19.0 0.7 copy.17
  19.7 0.1 reduce-window.9
  19.8 0.1 reduce
  19.9 0.7 subtract_multiply_fusion
  20.6 0.1 convert_reduce_fusion
  20.7 0.1 convert_reduce_fusion.1
  20.8 0.2 compare_and_fusion
  21.0 4.6 %copy.22 = bf16[128,16,512]{0,2,1:T(8,128)(2,1)} copy(bf16[128,16,512]{2,1,0:T(8,128)(2,1)} %param.6) | data formatting | bytes 4194304 | tf_op args[2]
  25.5 0.0 collective-permute-done
  25.6 1.7 %collective-permute-done.1 = bf16[128,576]{0,1:T(8,128)(2,1)S(1)} collective-permute-done((bf16[128,576]{0,1:T(8,128)(2,1)}, bf16[128,576]{0,1:T(8,128)(2,1)S(1)}, u32[]{:S(2)}, u32[]{:S(2)}) %collective-permute-start.1) | collective-permute-done | bytes 147488 | tf_op jit(solution)/shard_map/ppermute | solution.py:16
  27.3 0.7 collective-permute-done.2
  28.0 0.0 copy-done.2
  28.1 0.0 copy-done
  28.1 0.0 copy-start.1
  28.1 1.8 %fusion.20 = f32[512,128,16]{1,0,2:T(8,128)S(1)} fusion(bf16[128,16,576]{0,2,1:T(8,128)(2,1)S(1)} %copy-done, bf16[512,576]{0,1:T(8,128)(2,1)S(1)} %constant_dynamic-update-slice_fusion), kind=kOutput, calls=%fused_computation.27 | convolution fusion | flops 1207959552 | bytes 7143424 | tf_op jit(solution)/shard_map/thc,uc->htu/dot_general | solution.py:26
  30.0 0.0 copy-done.1
  30.0 3.3 %fusion.22 = f32[512,128,16]{1,0,2:T(8,128)} fusion(bf16[128,16,512]{0,2,1:T(8,128)(2,1)S(1)} %copy-done.1, bf16[512,576]{0,1:T(8,128)(2,1)S(1)} %constant_dynamic-update-slice_fusion), kind=kOutput, calls=%fused_computation.30 | convolution fusion | flops 1073741824 | bytes 6815744 | tf_op jit(solution)/shard_map/thc,uc->htu/dot_general | solution.py:34
  33.2 3.6 %fusion.33 = (f32[16,128]{1,0:T(8,128)S(1)}, f32[16,128,512]{1,2,0:T(8,128)}) fusion(f32[512,128,16]{1,0,2:T(8,128)S(1)} %fusion.20, pred[128,512]{0,1:T(8,128)(4,1)S(1)} %compare_and_fusion), kind=kOutput, calls=%fused_computation.52 | output fusion | flops 6291967 | bytes 8462336 | tf_op jit(solution)/shard_map/sub | solution.py:31
  36.8 7.4 %fusion.13 = f32[512,576]{0,1:T(8,128)S(1)} fusion(bf16[128,16,576]{0,2,1:T(8,128)(2,1)S(1)} %copy-done, f32[512,128,16]{1,0,2:T(8,128)} %fusion.22, f32[16,128,512]{1,2,0:T(8,128)} %get-tuple-element.9, f32[16,128]{1,0:T(8,128)S(1)} %get-tuple-element.8), kind=kOutput, calls=%fused_computation.21 | convolution fusion | flops 1215302144 | bytes 11935744 | tf_op jit(solution)/shard_map/htu,thc->uc/dot_general | solution.py:40
  44.2 4.2 %fusion.17 = f32[512,512]{0,1:T(8,128)S(1)} fusion(bf16[128,16,512]{0,2,1:T(8,128)(2,1)} %copy.22, f32[512,576]{0,1:T(8,128)S(1)} %fusion.13, f32[16,128,512]{1,2,0:T(8,128)} %get-tuple-element.9, f32[16,128]{1,0:T(8,128)S(1)} %get-tuple-element.8), kind=kOutput, calls=%fused_computation.23 | convolution fusion | flops 1076101120 | bytes 8396800 | tf_op jit(solution)/shard_map/htu,thc->uc/dot_general | solution.py:39
  48.4 0.1 fusion.28
  48.5 1.9 %collective-permute-start.3 = (f32[128,576]{0,1:T(8,128)S(1)}, f32[128,576]{0,1:T(8,128)S(1)}, u32[]{:S(2)}, u32[]{:S(2)}) collective-permute-start(f32[128,576]{0,1:T(8,128)S(1)} %get-tuple-element.5), channel_id=1, source_target_pairs={{4,0},{8,4},{12,8},{16,12},{20,16},{24,20},{28,24},{32,28},{36,32}... | collective-permute-start | bytes 884744 | tf_op jit(solution)/shard_map/ppermute | solution.py:16
  50.4 3.9 %collective-permute-start.4 = (f32[128,576]{0,1:T(8,128)S(1)}, f32[128,576]{0,1:T(8,128)S(1)}, u32[]{:S(2)}, u32[]{:S(2)}) collective-permute-start(f32[128,576]{0,1:T(8,128)S(1)} %get-tuple-element.7), channel_id=1, source_target_pairs={{8,0},{12,4},{16,8},{20,12},{24,16},{28,20},{32,24},{36,28},{40,32... | collective-permute-start | bytes 884744 | tf_op jit(solution)/shard_map/ppermute | solution.py:16
  54.3 3.1 %collective-permute-start.5 = (f32[128,576]{0,1:T(8,128)S(1)}, f32[128,576]{0,1:T(8,128)S(1)}, u32[]{:S(2)}, u32[]{:S(2)}) collective-permute-start(f32[128,576]{0,1:T(8,128)S(1)} %get-tuple-element.6), channel_id=1, source_target_pairs={{12,0},{16,4},{20,8},{24,12},{28,16},{32,20},{36,24},{40,28},{44,3... | collective-permute-start | bytes 884744 | tf_op jit(solution)/shard_map/ppermute | solution.py:16
  57.4 0.0 collective-permute-done.3
  57.4 10.0 %collective-permute-done.4 = f32[128,576]{0,1:T(8,128)S(1)} collective-permute-done((f32[128,576]{0,1:T(8,128)S(1)}, f32[128,576]{0,1:T(8,128)S(1)}, u32[]{:S(2)}, u32[]{:S(2)}) %collective-permute-start.4) | collective-permute-done | bytes 294944 | tf_op jit(solution)/shard_map/ppermute | solution.py:16
  67.4 3.1 %collective-permute-done.5 = f32[128,576]{0,1:T(8,128)S(1)} collective-permute-done((f32[128,576]{0,1:T(8,128)S(1)}, f32[128,576]{0,1:T(8,128)S(1)}, u32[]{:S(2)}, u32[]{:S(2)}) %collective-permute-start.5) | collective-permute-done | bytes 294944 | tf_op jit(solution)/shard_map/ppermute | solution.py:16
  70.5 0.8 fusion.27
  71.3 0.0 all-reduce.2.cloned.1.call-update
  71.3 54.3 %all-reduce.2.cloned.1.call-done = f32[128,576]{0,1:T(8,128)} async-done(((f32[128,576]{0,1:T(8,128)}), f32[128,576]{0,1:T(8,128)}) %all-reduce.2.cloned.1.call-update) | async-done | bytes 294928 | tf_op jit(solution)/shard_map/psum | solution.py:67
  125.6 1.7 %copy.31 = f32[128,576]{0,1:T(8,128)} copy(f32[128,576]{0,1:T(8,128)} %all-reduce.2.cloned.1.call-done) | data formatting | bytes 589824
  (7 shorter events, 0.2 us)
Async XLA Ops:
  6.5 21.5 %copy-start = (bf16[128,16,576]{0,2,1:T(8,128)(2,1)S(1)}, bf16[128,16,576]{0,2,1:T(8,128)(2,1)}, u32[]{:S(2)}) copy-start(bf16[128,16,576]{0,2,1:T(8,128)(2,1)} %param.4) | copy-start | bytes 7077892
  6.5 21.5 %copy-start.2 = (bf16[128,576]{0,1:T(8,128)(2,1)S(1)}, bf16[128,576]{0,1:T(8,128)(2,1)}, u32[]{:S(2)}) copy-start(bf16[128,576]{0,1:T(8,128)(2,1)} %param.5) | copy-start | bytes 442372
  6.5 119.1 %all-reduce.2.cloned.1.call-start = ((), (), s32[]{:S(2)}) async-start(), calls=%async_computation | async-start | bytes 589824 | tf_op jit(solution)/shard_map/psum | solution.py:67
  6.5 19.0 %collective-permute-start = (bf16[128,576]{0,1:T(8,128)(2,1)}, bf16[128,576]{0,1:T(8,128)(2,1)S(1)}, u32[]{:S(2)}, u32[]{:S(2)}) collective-permute-start(bf16[128,576]{0,1:T(8,128)(2,1)} %param.5), channel_id=1, source_target_pairs={{0,12},{4,16},{8,20},{12,24},{16,28},{20,32},{24,36},{28,40},{32,4... | collective-permute-start | bytes 442376 | tf_op jit(solution)/shard_map/ppermute | solution.py:16
  10.5 16.7 %collective-permute-start.1 = (bf16[128,576]{0,1:T(8,128)(2,1)}, bf16[128,576]{0,1:T(8,128)(2,1)S(1)}, u32[]{:S(2)}, u32[]{:S(2)}) collective-permute-start(bf16[128,576]{0,1:T(8,128)(2,1)} %param.5), channel_id=1, source_target_pairs={{0,8},{4,12},{8,16},{12,20},{16,24},{20,28},{24,32},{28,36},{32,40... | collective-permute-start | bytes 442376 | tf_op jit(solution)/shard_map/ppermute | solution.py:16
  14.8 13.2 %collective-permute-start.2 = (bf16[128,576]{0,1:T(8,128)(2,1)}, bf16[128,576]{0,1:T(8,128)(2,1)S(1)}, u32[]{:S(2)}, u32[]{:S(2)}) collective-permute-start(bf16[128,576]{0,1:T(8,128)(2,1)} %param.5), channel_id=1, source_target_pairs={{0,4},{4,8},{8,12},{12,16},{16,20},{20,24},{24,28},{28,32},{32,36}... | collective-permute-start | bytes 442376 | tf_op jit(solution)/shard_map/ppermute | solution.py:16
  28.1 1.9 %copy-start.1 = (bf16[128,16,512]{0,2,1:T(8,128)(2,1)S(1)}, bf16[128,16,512]{0,2,1:T(8,128)(2,1)}, u32[]{:S(2)}) copy-start(bf16[128,16,512]{0,2,1:T(8,128)(2,1)} %copy.22) | copy-start | bytes 6291460
  48.5 8.9 %collective-permute-start.3 = (f32[128,576]{0,1:T(8,128)S(1)}, f32[128,576]{0,1:T(8,128)S(1)}, u32[]{:S(2)}, u32[]{:S(2)}) collective-permute-start(f32[128,576]{0,1:T(8,128)S(1)} %get-tuple-element.5), channel_id=1, source_target_pairs={{4,0},{8,4},{12,8},{16,12},{20,16},{24,20},{28,24},{32,28},{36,32}... | collective-permute-start | bytes 884744 | tf_op jit(solution)/shard_map/ppermute | solution.py:16
  50.4 17.0 %collective-permute-start.4 = (f32[128,576]{0,1:T(8,128)S(1)}, f32[128,576]{0,1:T(8,128)S(1)}, u32[]{:S(2)}, u32[]{:S(2)}) collective-permute-start(f32[128,576]{0,1:T(8,128)S(1)} %get-tuple-element.7), channel_id=1, source_target_pairs={{8,0},{12,4},{16,8},{20,12},{24,16},{28,20},{32,24},{36,28},{40,32... | collective-permute-start | bytes 884744 | tf_op jit(solution)/shard_map/ppermute | solution.py:16
  54.3 16.2 %collective-permute-start.5 = (f32[128,576]{0,1:T(8,128)S(1)}, f32[128,576]{0,1:T(8,128)S(1)}, u32[]{:S(2)}, u32[]{:S(2)}) collective-permute-start(f32[128,576]{0,1:T(8,128)S(1)} %get-tuple-element.6), channel_id=1, source_target_pairs={{12,0},{16,4},{20,8},{24,12},{28,16},{32,20},{36,24},{40,28},{44,3... | collective-permute-start | bytes 884744 | tf_op jit(solution)/shard_map/ppermute | solution.py:16
Sparse Core Ops, SparseCore 0:
  71.4 54.1 all-reduce.1
where the time goes:
time: 135 us; the launch traced here: 134 us
  waiting for transfers between devices  69.8 us (52%)
  starting transfers between devices  21.2 us (16%)
  matrix products  16.7 us (12%)
  between operations  13.6 us (10%)
  local copies, waits for them, and re-layouts  7.16 us (5%)
  other arithmetic  5.73 us (4%)
    psum x1, waiting for transfers between devices, shards(): result = lax.psum(summed, 'head')  54.3 us
    ppermute x6, starting transfers between devices, passed_along(): return lax.ppermute(x, axis, pairs)  21.2 us
    ppermute x6, waiting for transfers between devices, passed_along(): return lax.ppermute(x, axis, pairs)  15.4 us
    dot_general x1, matrix products, window_grads(): jnp.einsum('htu,thc->uc', grad_scores, query_rows, preferred_element_type...  7.39 us
    unnamed x11, local copies, waits for them, and re-layouts  6.36 us
    dot_general x1, matrix products, window_grads(): jnp.einsum('htu,thc->uc', probs_low, grad_rows, preferred_element_type=jn...  4.16 us
    sub x1, other arithmetic, window_grads(): raised = jnp.exp(scores - row_max)  3.59 us
    dot_general x1, matrix products, window_grads(): jnp.einsum('thc,uc->htu', grad_rows, window[:, :lat_width], preferred_ele...  3.28 us
  transfers between devices with their start and end apart: 7, of which 5 were waited for; matrix products, arithmetic and copies ran while one was open for 5% of the time, Pallas kernels for 0%

commit v1 on v0

v1 whole, which is shorter than its diff:
```python
import jax
import jax.numpy as jnp
from jax import lax
from jax.experimental import pallas as pl
from jax.experimental.pallas import tpu as pltpu
from jax.sharding import PartitionSpec as P

BLOCK = 128
BACK = 3
GROUP = 4

softmax_scale = 192.0 ** (-0.5)


def passed_along(x, axis, by):
    peers = lax.axis_size(axis)
    pairs = [(i, i + by) for i in range(peers) if 0 <= i + by < peers]
    return lax.ppermute(x, axis, pairs)


def blocks_back(doc_blocks, block):
    count = doc_blocks.shape[0]
    earlier = jnp.arange(count)[:, None] > jnp.arange(count)[None, :]
    starts = jnp.sum(jnp.where(earlier, doc_blocks[None, :], 0), axis=1)
    first = jnp.max(jnp.where(starts <= block, starts, 0))
    return (block - first).astype(jnp.int32).reshape(1)


def grads_kernel(back_ref, q_ref, g_ref, k3_ref, k2_ref, k1_ref, k0_ref, far_ref, own_ref, keys, total):
    step = pl.program_id(0)
    span, width = keys.shape
    lat = g_ref.shape[1]
    blk = k0_ref.shape[1]

    @pl.when(step == 0)
    def _():
        for j, ref in enumerate((k3_ref, k2_ref, k1_ref, k0_ref)):
            keys[j * blk:(j + 1) * blk, :] = ref[...].T

    q = jnp.concatenate([q_ref[h] for h in range(GROUP)], axis=1)
    g = jnp.concatenate([g_ref[h] for h in range(GROUP)], axis=1)
    cols = q.shape[1]
    window = keys[...]
    scores = jnp.dot(window, q, preferred_element_type=jnp.float32) * softmax_scale
    grad_probs = jnp.dot(window[:, :lat], g, preferred_element_type=jnp.float32)
    row = lax.broadcasted_iota(jnp.int32, (span, cols), 0)
    col = lax.broadcasted_iota(jnp.int32, (span, cols), 1)
    first = (BACK - back_ref[0]) * blk
    visible = (row >= first) & (row <= BACK * blk + (col & (blk - 1)))
    scores = jnp.where(visible, scores, -jnp.inf)
    raised = jnp.exp(scores - jnp.max(scores, axis=0, keepdims=True))
    probs = raised * (1.0 / jnp.sum(raised, axis=0, keepdims=True))
    dot = jnp.sum(probs * grad_probs, axis=0, keepdims=True)
    grad_scores = (probs * (grad_probs - dot) * softmax_scale).astype(jnp.bfloat16)
    low = probs.astype(jnp.bfloat16)
    nt = (((1,), (1,)), ((), ()))
    upper = lax.dot_general(
        jnp.concatenate([q[:lat], g], axis=1),
        jnp.concatenate([grad_scores, low], axis=1),
        nt, preferred_element_type=jnp.float32)
    lower = lax.dot_general(q[lat:], grad_scores, nt, preferred_element_type=jnp.float32)

    @pl.when(step == 0)
    def _():
        total[:lat, :] = upper
        total[lat:, :] = lower

    @pl.when(step > 0)
    def _():
        total[:lat, :] += upper
        total[lat:, :] += lower

    @pl.when(step == pl.num_programs(0) - 1)
    def _():
        for j in range(BACK):
            far_ref[j] = total[:, j * blk:(j + 1) * blk].astype(far_ref.dtype)
        own_ref[...] = total[:, BACK * blk:]


def window_grads(back, q, g, keys):
    heads, width, rows = q.shape
    lat = g.shape[1]
    whole = pl.BlockSpec((width, rows), lambda i: (0, 0))
    return pl.pallas_call(
        grads_kernel,
        grid=(heads // GROUP,),
        in_specs=[
            pl.BlockSpec(memory_space=pltpu.SMEM),
            pl.BlockSpec((GROUP, width, rows), lambda i: (i, 0, 0)),
            pl.BlockSpec((GROUP, lat, rows), lambda i: (i, 0, 0)),
            whole, whole, whole, whole,
        ],
        out_specs=[pl.BlockSpec((BACK, width, rows), lambda i: (0, 0, 0)), whole],
        out_shape=[
            jax.ShapeDtypeStruct((BACK, width, rows), jnp.bfloat16),
            jax.ShapeDtypeStruct((width, rows), jnp.float32),
        ],
        scratch_shapes=[
            pltpu.VMEM(((BACK + 1) * rows, width), jnp.bfloat16),
            pltpu.VMEM((width, (BACK + 1) * rows), jnp.float32),
        ],
        compiler_params=pltpu.CompilerParams(vmem_limit_bytes=40 * 1024 * 1024),
        name="window_grads",
    )(back, q, g, *keys)


def shards(queries, latent, out_grad, doc_blocks):
    own = latent.T
    keys = [passed_along(own, "ctx", offset) for offset in range(BACK, 0, -1)] + [own]
    back = blocks_back(doc_blocks, lax.axis_index("ctx"))
    q = jnp.transpose(queries, (1, 2, 0))
    g = jnp.transpose(out_grad, (1, 2, 0))
    far, near = window_grads(back, q, g, keys)
    for offset in range(BACK, 0, -1):
        near = near + passed_along(far[BACK - offset], "ctx", -offset).astype(jnp.float32)
    low = near.astype(jnp.bfloat16)
    heads = lax.axis_size("head")
    spread = jnp.broadcast_to(low[None], (heads,) + low.shape)
    parts = lax.all_to_all(spread, "head", 0, 0, tiled=True)
    return jnp.sum(parts.astype(jnp.float32), axis=0).T


def solution(mesh):
    return jax.shard_map(
        shards,
        mesh=mesh,
        in_specs=(P("ctx", "head", None), P("ctx", None), P("ctx", "head", None), P()),
        out_specs=P("ctx", None),
        check_vma=False,
    )
```

time: 135 us -> 63.2 us (0.47)
  the two profiles are of different devices: /device:TPU:8 before, /device:TPU:48 now
where the time goes in v1:
time: 63.2 us; the launch traced here: 62.8 us
  starting transfers between devices  24.3 us (38%)
  blocking collectives  14.2 us (22%)
  Pallas kernels  8.8 us (14%)
  waiting for transfers between devices  7.12 us (11%)
  local copies, waits for them, and re-layouts  5.3 us (8%)
  other arithmetic  2.28 us (4%)
  between operations  0.77 us (1%)
    ppermute x6, starting transfers between devices, passed_along(): return lax.ppermute(x, axis, pairs)  24.3 us
    all_to_all x1, blocking collectives, shards(): parts = lax.all_to_all(spread, 'head', 0, 0, tiled=True)  14.2 us
    pallas_call x1, Pallas kernels, window_grads(): pl.pallas_call(grads_kernel, grid=(heads // GROUP,), in_specs=[pl.BlockSp...  8.8 us
    ppermute x6, waiting for transfers between devices, passed_along(): return lax.ppermute(x, axis, pairs)  7.12 us
    unnamed x5, local copies, waits for them, and re-layouts  5.19 us
  transfers between devices with their start and end apart: 6, of which 4 were waited for; matrix products, arithmetic and copies ran while one was open for 8% of the time, Pallas kernels for 0%

profile of v1, /device:TPU:48, one launch (start us, length us, event | category | flops | bytes accessed | tf_op | source)
XLA Modules:
  0.0 62.8 jit_solution(16995814159916475932)
XLA Ops:
  0.0 1.9 %collective-permute-start.2 = (bf16[576,128]{1,0:T(8,128)(2,1)}, bf16[576,128]{1,0:T(8,128)(2,1)S(1)}, u32[]{:S(2)}, u32[]{:S(2)}) collective-permute-start(bf16[576,128]{1,0:T(8,128)(2,1)} %bitcast.13), channel_id=1, source_target_pairs={{0,4},{4,8},{8,12},{12,16},{16,20},{20,24},{24,28},{28,32},{32,36}... | collective-permute-start | bytes 442376 | tf_op jit(solution)/shard_map/ppermute | solution.py:18
  1.9 4.3 %collective-permute-start.1 = (bf16[576,128]{1,0:T(8,128)(2,1)}, bf16[576,128]{1,0:T(8,128)(2,1)S(1)}, u32[]{:S(2)}, u32[]{:S(2)}) collective-permute-start(bf16[576,128]{1,0:T(8,128)(2,1)} %bitcast.14), channel_id=1, source_target_pairs={{0,8},{4,12},{8,16},{12,20},{16,24},{20,28},{24,32},{28,36},{32,40... | collective-permute-start | bytes 442376 | tf_op jit(solution)/shard_map/ppermute | solution.py:18
  6.2 6.1 %collective-permute-start = (bf16[576,128]{1,0:T(8,128)(2,1)}, bf16[576,128]{1,0:T(8,128)(2,1)S(1)}, u32[]{:S(2)}, u32[]{:S(2)}) collective-permute-start(bf16[576,128]{1,0:T(8,128)(2,1)} %bitcast.15), channel_id=1, source_target_pairs={{0,12},{4,16},{8,20},{12,24},{16,28},{20,32},{24,36},{28,40},{32,4... | collective-permute-start | bytes 442376 | tf_op jit(solution)/shard_map/ppermute | solution.py:18
  12.3 0.8 %select_reduce_fusion = s32[64]{0:T(128)S(1)} fusion(s32[64]{0:T(128)} %param.7), kind=kLoop, calls=%fused_computation.5 | loop fusion | flops 12224 | bytes 512 | tf_op jit(solution)/shard_map/reduce_sum | solution.py:24
  13.1 0.6 %fusion = s32[]{:T(128)} fusion(s32[64]{0:T(128)S(1)} %select_reduce_fusion, s32[]{:T(128)S(6)} %axis_index.15), kind=kLoop, calls=%fused_computation.8 | loop fusion | flops 191 | bytes 264 | tf_op jit(solution)/shard_map/reduce_max | solution.py:25
  14.4 0.0 copy-start.1
  14.4 3.5 %copy.6 = bf16[128,16,512]{0,2,1:T(8,128)(2,1)S(1)} copy(bf16[128,16,512]{2,1,0:T(8,128)(2,1)} %param.6) | data formatting | bytes 4194304 | tf_op args[2]
  17.9 0.0 collective-permute-done.2.k1_ref
  17.9 0.9 %collective-permute-done.1.k2_ref = bf16[576,128]{1,0:T(8,128)(2,1)S(1)} collective-permute-done((bf16[576,128]{1,0:T(8,128)(2,1)}, bf16[576,128]{1,0:T(8,128)(2,1)S(1)}, u32[]{:S(2)}, u32[]{:S(2)}) %collective-permute-start.1) | collective-permute-done | bytes 147488 | tf_op jit(solution)/shard_map/ppermute | solution.py:18
  18.8 2.5 %collective-permute-done.k3_ref = bf16[576,128]{1,0:T(8,128)(2,1)S(1)} collective-permute-done((bf16[576,128]{1,0:T(8,128)(2,1)}, bf16[576,128]{1,0:T(8,128)(2,1)S(1)}, u32[]{:S(2)}, u32[]{:S(2)}) %collective-permute-start) | collective-permute-done | bytes 147488 | tf_op jit(solution)/shard_map/ppermute | solution.py:18
  21.3 0.0 copy-done.1
  21.3 0.0 copy-start
  21.3 1.7 %copy-done = bf16[128,16,576]{0,2,1:T(8,128)(2,1)S(1)} copy-done((bf16[128,16,576]{0,2,1:T(8,128)(2,1)S(1)}, bf16[128,16,576]{0,2,1:T(8,128)(2,1)}, u32[]{:S(2)}) %copy-start) | copy-done | bytes 2359320
  22.9 8.8 %window_grads.1 = (bf16[3,576,128]{2,1,0:T(8,128)(2,1)S(1)}, f32[576,128]{1,0:T(8,128)S(1)}) custom-call(s32[1]{0:T(128)} %bitcast.back_ref, bf16[16,576,128]{2,1,0:T(8,128)(2,1)S(1)} %bitcast.12, bf16[16,512,128]{2,1,0:T(8,128)(2,1)S(1)} %bitcast.11, bf16[576,128]{1,0:T(8,128)(2,1)S(1)} %collective-permute-done.k3_ref, ...), custom_call_target="tpu_custom_call" | custom-call | tf_op jit(solution)/shard_map/window_grads/pallas_call | solution.py:84
  31.8 5.4 %collective-permute-start.3 = (bf16[576,128]{1,0:T(8,128)(2,1)S(1)}, bf16[576,128]{1,0:T(8,128)(2,1)S(1)}, u32[]{:S(2)}, u32[]{:S(2)}) collective-permute-start(bf16[576,128]{1,0:T(8,128)(2,1)S(1)} %get-tuple-element.9), channel_id=1, source_target_pairs={{12,0},{16,4},{20,8},{24,12},{28,16},{32,20},{36,24},{40,28},{44,3... | collective-permute-start | bytes 442376 | tf_op jit(solution)/shard_map/ppermute | solution.py:18
  37.2 2.2 %collective-permute-start.5 = (bf16[576,128]{1,0:T(8,128)(2,1)S(1)}, bf16[576,128]{1,0:T(8,128)(2,1)S(1)}, u32[]{:S(2)}, u32[]{:S(2)}) collective-permute-start(bf16[576,128]{1,0:T(8,128)(2,1)S(1)} %get-tuple-element.10), channel_id=1, source_target_pairs={{4,0},{8,4},{12,8},{16,12},{20,16},{24,20},{28,24},{32,28},{36,32}... | collective-permute-start | bytes 442376 | tf_op jit(solution)/shard_map/ppermute | solution.py:18
  39.4 4.5 %collective-permute-start.4 = (bf16[576,128]{1,0:T(8,128)(2,1)S(1)}, bf16[576,128]{1,0:T(8,128)(2,1)S(1)}, u32[]{:S(2)}, u32[]{:S(2)}) collective-permute-start(bf16[576,128]{1,0:T(8,128)(2,1)S(1)} %get-tuple-element.11), channel_id=1, source_target_pairs={{8,0},{12,4},{16,8},{20,12},{24,16},{28,20},{32,24},{36,28},{40,32... | collective-permute-start | bytes 442376 | tf_op jit(solution)/shard_map/ppermute | solution.py:18
  43.9 0.0 collective-permute-done.3
  43.9 2.2 %collective-permute-done.5 = bf16[576,128]{1,0:T(8,128)(2,1)S(1)} collective-permute-done((bf16[576,128]{1,0:T(8,128)(2,1)S(1)}, bf16[576,128]{1,0:T(8,128)(2,1)S(1)}, u32[]{:S(2)}, u32[]{:S(2)}) %collective-permute-start.5) | collective-permute-done | bytes 147488 | tf_op jit(solution)/shard_map/ppermute | solution.py:18
  46.1 1.6 %collective-permute-done.4 = bf16[576,128]{1,0:T(8,128)(2,1)S(1)} collective-permute-done((bf16[576,128]{1,0:T(8,128)(2,1)S(1)}, bf16[576,128]{1,0:T(8,128)(2,1)S(1)}, u32[]{:S(2)}, u32[]{:S(2)}) %collective-permute-start.4) | collective-permute-done | bytes 147488 | tf_op jit(solution)/shard_map/ppermute | solution.py:18
  47.6 0.1 add_convert_fusion
  47.7 0.1 broadcast_in_dim.28
  47.8 14.2 %all_to_all.5 = bf16[4,576,128]{2,1,0:T(8,128)(2,1)S(1)} all-to-all(bf16[4,576,128]{2,1,0:T(8,128)(2,1)S(1)} %broadcast_in_dim.28), channel_id=1, replica_groups=mesh['ctx'=128,'head'=4] {'head'}, dimensions={0} | all-to-all | bytes 1179648 | tf_op jit(solution)/shard_map/all_to_all | solution.py:119
  62.0 0.8 %convert_reduce_fusion = f32[576,128]{1,0:T(8,128)} fusion(bf16[4,576,128]{2,1,0:T(8,128)(2,1)S(1)} %all_to_all.5), kind=kLoop, calls=%fused_computation | loop fusion | flops 516096 | bytes 884736 | tf_op jit(solution)/shard_map/reduce_sum | solution.py:120
  (1 shorter events, 0.0 us)
Async XLA Ops:
  0.0 17.9 %collective-permute-start.2 = (bf16[576,128]{1,0:T(8,128)(2,1)}, bf16[576,128]{1,0:T(8,128)(2,1)S(1)}, u32[]{:S(2)}, u32[]{:S(2)}) collective-permute-start(bf16[576,128]{1,0:T(8,128)(2,1)} %bitcast.13), channel_id=1, source_target_pairs={{0,4},{4,8},{8,12},{12,16},{16,20},{20,24},{24,28},{28,32},{32,36}... | collective-permute-start | bytes 442376 | tf_op jit(solution)/shard_map/ppermute | solution.py:18
  1.9 16.9 %collective-permute-start.1 = (bf16[576,128]{1,0:T(8,128)(2,1)}, bf16[576,128]{1,0:T(8,128)(2,1)S(1)}, u32[]{:S(2)}, u32[]{:S(2)}) collective-permute-start(bf16[576,128]{1,0:T(8,128)(2,1)} %bitcast.14), channel_id=1, source_target_pairs={{0,8},{4,12},{8,16},{12,20},{16,24},{20,28},{24,32},{28,36},{32,40... | collective-permute-start | bytes 442376 | tf_op jit(solution)/shard_map/ppermute | solution.py:18
  6.2 15.1 %collective-permute-start = (bf16[576,128]{1,0:T(8,128)(2,1)}, bf16[576,128]{1,0:T(8,128)(2,1)S(1)}, u32[]{:S(2)}, u32[]{:S(2)}) collective-permute-start(bf16[576,128]{1,0:T(8,128)(2,1)} %bitcast.15), channel_id=1, source_target_pairs={{0,12},{4,16},{8,20},{12,24},{16,28},{20,32},{24,36},{28,40},{32,4... | collective-permute-start | bytes 442376 | tf_op jit(solution)/shard_map/ppermute | solution.py:18
  14.4 6.9 %copy-start.1 = (bf16[128,576]{0,1:T(8,128)(2,1)S(1)}, bf16[128,576]{0,1:T(8,128)(2,1)}, u32[]{:S(2)}) copy-start(bf16[128,576]{0,1:T(8,128)(2,1)} %param.5) | copy-start | bytes 442372
  21.3 1.7 %copy-start = (bf16[128,16,576]{0,2,1:T(8,128)(2,1)S(1)}, bf16[128,16,576]{0,2,1:T(8,128)(2,1)}, u32[]{:S(2)}) copy-start(bf16[128,16,576]{0,2,1:T(8,128)(2,1)} %param.4) | copy-start | bytes 7077892
  31.8 12.1 %collective-permute-start.3 = (bf16[576,128]{1,0:T(8,128)(2,1)S(1)}, bf16[576,128]{1,0:T(8,128)(2,1)S(1)}, u32[]{:S(2)}, u32[]{:S(2)}) collective-permute-start(bf16[576,128]{1,0:T(8,128)(2,1)S(1)} %get-tuple-element.9), channel_id=1, source_target_pairs={{12,0},{16,4},{20,8},{24,12},{28,16},{32,20},{36,24},{40,28},{44,3... | collective-permute-start | bytes 442376 | tf_op jit(solution)/shard_map/ppermute | solution.py:18
  37.2 8.9 %collective-permute-start.5 = (bf16[576,128]{1,0:T(8,128)(2,1)S(1)}, bf16[576,128]{1,0:T(8,128)(2,1)S(1)}, u32[]{:S(2)}, u32[]{:S(2)}) collective-permute-start(bf16[576,128]{1,0:T(8,128)(2,1)S(1)} %get-tuple-element.10), channel_id=1, source_target_pairs={{4,0},{8,4},{12,8},{16,12},{20,16},{24,20},{28,24},{32,28},{36,32}... | collective-permute-start | bytes 442376 | tf_op jit(solution)/shard_map/ppermute | solution.py:18
  39.4 8.2 %collective-permute-start.4 = (bf16[576,128]{1,0:T(8,128)(2,1)S(1)}, bf16[576,128]{1,0:T(8,128)(2,1)S(1)}, u32[]{:S(2)}, u32[]{:S(2)}) collective-permute-start(bf16[576,128]{1,0:T(8,128)(2,1)S(1)} %get-tuple-element.11), channel_id=1, source_target_pairs={{8,0},{12,4},{16,8},{20,12},{24,16},{28,20},{32,24},{36,28},{40,32... | collective-permute-start | bytes 442376 | tf_op jit(solution)/shard_map/ppermute | solution.py:18

commit v2 on v0

v2 whole, which is shorter than its diff:
```python
import math

import jax
import jax.numpy as jnp
from jax import lax
from jax.experimental import pallas as pl
from jax.experimental.pallas import tpu as pltpu
from jax.sharding import PartitionSpec as P

BLOCK = 128
GROUP = 8
LANES = 128
OWN_FLOPS = 4 * 10 ** 9

softmax_scale = 192.0 ** (-0.5)
to_exponent = softmax_scale * math.log2(math.e)
NT = (((1,), (1,)), ((), ()))
VMEM = pl.BlockSpec(memory_space=pltpu.VMEM)
SMEM = pl.BlockSpec(memory_space=pltpu.SMEM)


def skip_pairs(n):
    ahead = [(i, i + 1 if i % 2 == 0 else i + 3) for i in range(n)]
    return [(i, j) for i, j in ahead if j < n]


def step_pairs(n):
    return [(i, i + 2) for i in range(n - 2)]


def swap_pairs(n):
    return [(i, i ^ 1) for i in range(n)]


def turned(pairs):
    return [(j, i) for i, j in pairs]


def side_by_side(ref, at):
    return jnp.concatenate([ref[at + h] for h in range(GROUP)], axis=1)


def own_kernel(shard_ref, docs_ref, g_ref, own_ref, seen_ref, grads_ref):
    heads, lat, blk = g_ref.shape

    docs = docs_ref[...]
    square = (docs.shape[1], docs.shape[1])
    earlier = lax.broadcasted_iota(jnp.int32, square, 1) < lax.broadcasted_iota(jnp.int32, square, 0)
    starts = jnp.sum(jnp.where(earlier, docs, 0), axis=1, keepdims=True)
    shard = shard_ref[0]
    first = jnp.max(jnp.where(starts <= shard, starts, 0), axis=0, keepdims=True)
    even = lax.rem(shard, 2) == 0
    slot = lax.broadcasted_iota(jnp.int32, seen_ref.shape, 0)
    offset = jnp.where(slot == 0, jnp.where(even, 1, 3), jnp.where(slot == 1, jnp.where(even, 3, 1), 2))
    seen_ref[...] = (offset <= shard - first).astype(jnp.int32)

    rows = own_ref[:lat, :].T
    for at in range(0, heads, GROUP):
        grads_ref[:, at * blk:(at + GROUP) * blk] = jnp.dot(
            rows, side_by_side(g_ref, at), preferred_element_type=jnp.float32)


def own_grads(shard, doc_blocks, g, own):
    heads, lat, rows = g.shape
    return pl.pallas_call(
        own_kernel,
        in_specs=[SMEM] + [VMEM] * 3, out_specs=[VMEM, VMEM],
        out_shape=[
            jax.ShapeDtypeStruct((8, LANES), jnp.int32),
            jax.ShapeDtypeStruct((rows, heads * rows), jnp.float32),
        ],
        compiler_params=pltpu.CompilerParams(vmem_limit_bytes=30 * 1024 * 1024),
        cost_estimate=pl.CostEstimate(flops=OWN_FLOPS, bytes_accessed=0, transcendentals=0),
        name="own_grads",
    )(shard, doc_blocks, g, own)


def products_kernel(q_ref, g_ref, step_ref, own_ref, scores_ref, grads_ref):
    heads, lat, blk = g_ref.shape
    rows = jnp.concatenate([step_ref[...].T, own_ref[...].T], axis=0)
    for at in range(0, heads, GROUP):
        where = slice(at * blk, (at + GROUP) * blk)
        scores = jnp.dot(rows, side_by_side(q_ref, at), preferred_element_type=jnp.float32)
        key = lax.broadcasted_iota(jnp.int32, scores[blk:].shape, 0)
        query = lax.broadcasted_iota(jnp.int32, scores[blk:].shape, 1) & (blk - 1)
        scores_ref[:blk, where] = scores[:blk]
        scores_ref[blk:, where] = jnp.where(key <= query, scores[blk:], -jnp.inf)
        grads_ref[:, where] = jnp.dot(
            rows[:blk, :lat], side_by_side(g_ref, at), preferred_element_type=jnp.float32)


def products(q, g, step, own):
    heads, width, rows = q.shape
    return pl.pallas_call(
        products_kernel,
        in_specs=[VMEM] * 4, out_specs=[VMEM, VMEM],
        out_shape=[
            jax.ShapeDtypeStruct((2 * rows, heads * rows), jnp.float32),
            jax.ShapeDtypeStruct((rows, heads * rows), jnp.float32),
        ],
        compiler_params=pltpu.CompilerParams(vmem_limit_bytes=30 * 1024 * 1024),
        name="products",
    )(q, g, step, own)


def transposed_sums(q, g, grad_scores, low):
    lat = g.shape[0]
    upper = lax.dot_general(
        jnp.concatenate([q[:lat], g], axis=1), jnp.concatenate([grad_scores, low], axis=1),
        NT, preferred_element_type=jnp.float32)
    lower = lax.dot_general(q[lat:], grad_scores, NT, preferred_element_type=jnp.float32)
    return upper, lower


def put(refs, upper, lower):
    lat = upper.shape[0]
    for j, ref in enumerate(refs):
        blk = ref.shape[1]
        ref[:lat, :] = upper[:, j * blk:(j + 1) * blk].astype(ref.dtype)
        ref[lat:, :] = lower[:, j * blk:(j + 1) * blk].astype(ref.dtype)


def first_kernel(seen_ref, q_ref, g_ref, swap_ref, skip_ref, near_s, step_g, own_g,
                 swap_out, skip_out, scores_out, low_out):
    heads, lat, blk = g_ref.shape
    rows = jnp.concatenate([swap_ref[...].T, skip_ref[...].T], axis=0)
    upper = lower = None
    for at in range(0, heads, GROUP):
        where = pl.ds(at * blk, GROUP * blk)
        q = side_by_side(q_ref, at)
        g = side_by_side(g_ref, at)
        scores = jnp.dot(rows, q, preferred_element_type=jnp.float32)
        grad_probs = jnp.dot(rows[:, :lat], g, preferred_element_type=jnp.float32)
        grad_probs = jnp.concatenate([grad_probs, step_g[:, where], own_g[:, where]], axis=0)
        parts = [scores[:blk], scores[blk:], near_s[:blk, where], near_s[blk:, where]]
        tops = [jnp.max(part, axis=0, keepdims=True) for part in parts]
        top = tops[3]
        for j in range(3):
            top = jnp.maximum(top, jnp.where(seen_ref[j:j + 1, :1] > 0, tops[j], -jnp.inf))
        top = top * to_exponent
        less = [jnp.where(seen_ref[j:j + 1, :1] > 0, top, jnp.inf) for j in range(3)] + [top]
        raised = jnp.concatenate([jnp.exp2(p * to_exponent - b) for p, b in zip(parts, less)], axis=0)
        inverse = 1.0 / jnp.sum(raised, axis=0, keepdims=True)
        dot = jnp.sum(raised * grad_probs, axis=0, keepdims=True) * inverse
        low = (raised * inverse).astype(jnp.bfloat16)
        grad_scores = ((raised * (inverse * softmax_scale)) * (grad_probs - dot)).astype(jnp.bfloat16)
        scores_out[:, where] = grad_scores[2 * blk:]
        low_out[:, where] = low[2 * blk:]
        up, down = transposed_sums(q, g, grad_scores[:2 * blk], low[:2 * blk])
        upper = up if upper is None else upper + up
        lower = down if lower is None else lower + down
    put((swap_out, skip_out), upper, lower)


def first_grads(seen, q, g, swap, skip, near_scores, step_grads, own_grads):
    heads, width, rows = q.shape
    sent = jax.ShapeDtypeStruct((width, rows), jnp.bfloat16)
    kept = jax.ShapeDtypeStruct((2 * rows, heads * rows), jnp.bfloat16)
    return pl.pallas_call(
        first_kernel,
        in_specs=[VMEM] * 8, out_specs=[VMEM] * 4, out_shape=[sent, sent, kept, kept],
        compiler_params=pltpu.CompilerParams(vmem_limit_bytes=30 * 1024 * 1024),
        name="first_grads",
    )(seen, q, g, swap, skip, near_scores, step_grads, own_grads)


def second_kernel(q_ref, g_ref, scores_ref, low_ref, step_out, own_out):
    heads, lat, blk = g_ref.shape
    upper = lower = None
    for at in range(0, heads, GROUP):
        where = pl.ds(at * blk, GROUP * blk)
        up, down = transposed_sums(
            side_by_side(q_ref, at), side_by_side(g_ref, at), scores_ref[:, where], low_ref[:, where])
        upper = up if upper is None else upper + up
        lower = down if lower is None else lower + down
    put((step_out, own_out), upper, lower)


def second_grads(q, g, grad_scores, low):
    heads, width, rows = q.shape
    made = jax.ShapeDtypeStruct((width, rows), jnp.float32)
    return pl.pallas_call(
        second_kernel,
        in_specs=[VMEM] * 4, out_specs=[VMEM] * 2, out_shape=[made, made],
        compiler_params=pltpu.CompilerParams(vmem_limit_bytes=30 * 1024 * 1024),
        name="second_grads",
    )(q, g, grad_scores, low)


def after(x, *others):
    return lax.optimization_barrier((x,) + others)[0]


def shards(queries, latent, out_grad, doc_blocks):
    n = lax.axis_size("ctx")
    shard = lax.axis_index("ctx")
    own = latent.T
    step = lax.ppermute(own, "ctx", step_pairs(n))
    skip = lax.ppermute(own, "ctx", skip_pairs(n))
    q = jnp.transpose(queries, (1, 2, 0))
    g = jnp.transpose(out_grad, (1, 2, 0))
    seen, of_own = own_grads(shard.reshape(1), doc_blocks.reshape(1, -1), g, own)
    step = after(step, of_own)
    swap = lax.ppermute(step, "ctx", swap_pairs(n))
    near_scores, of_step = products(q, g, step, own)
    swap, skip, grad_scores, low = first_grads(seen, q, g, swap, skip, near_scores, of_step, of_own)
    swap = lax.ppermute(swap, "ctx", swap_pairs(n))
    skip = lax.ppermute(skip, "ctx", turned(skip_pairs(n)))
    step, near = second_grads(q, g, grad_scores, low)
    step = (step + swap.astype(jnp.float32)).astype(jnp.bfloat16)
    step = lax.ppermute(step, "ctx", turned(step_pairs(n)))
    low = (near + skip.astype(jnp.float32) + step.astype(jnp.float32)).astype(jnp.bfloat16)
    heads = lax.axis_size("head")
    spread = jnp.broadcast_to(low[None], (heads,) + low.shape)
    parts = lax.all_to_all(spread, "head", 0, 0, tiled=True)
    return jnp.sum(parts.astype(jnp.float32), axis=0).T


def solution(mesh):
    return jax.shard_map(
        shards,
        mesh=mesh,
        in_specs=(P("ctx", "head", None), P("ctx", None), P("ctx", "head", None), P()),
        out_specs=P("ctx", None),
        check_vma=False,
    )
```

time: 135 us -> 56.8 us (0.42)
  the two profiles are of different devices: /device:TPU:8 before, /device:TPU:24 now
where the time goes in v2:
time: 56.8 us; the launch traced here: 56.4 us
  starting transfers between devices  17.6 us (31%)
  blocking collectives  13.5 us (24%)
  waiting for transfers between devices  12.8 us (23%)
  Pallas kernels  7.89 us (14%)
  local copies, waits for them, and re-layouts  3.62 us (6%)
  other arithmetic  0.88 us (2%)
    all_to_all x1, blocking collectives, shards(): parts = lax.all_to_all(spread, 'head', 0, 0, tiled=True)  13.5 us
    ppermute x1, waiting for transfers between devices, shards(): step = lax.ppermute(own, 'ctx', step_pairs(n))  7.74 us
    ppermute x1, waiting for transfers between devices, shards(): step = lax.ppermute(step, 'ctx', turned(step_pairs(n)))  5.06 us
    pallas_call x1, Pallas kernels, first_grads(): pl.pallas_call(first_kernel, in_specs=[VMEM] * 8, out_specs=[VMEM] * 4, o...  4.56 us
    ppermute x1, starting transfers between devices, shards(): skip = lax.ppermute(skip, 'ctx', turned(skip_pairs(n)))  4.53 us
    ppermute x1, starting transfers between devices, shards(): step = lax.ppermute(own, 'ctx', step_pairs(n))  4.28 us
    unnamed x7, local copies, waits for them, and re-layouts  3.54 us
    ppermute x1, starting transfers between devices, shards(): step = lax.ppermute(step, 'ctx', turned(step_pairs(n)))  2.54 us
  transfers between devices with their start and end apart: 6, of which 2 were waited for; matrix products, arithmetic and copies ran while one was open for 6% of the time, Pallas kernels for 6%

profile of v2, /device:TPU:24, one launch (start us, length us, event | category | flops | bytes accessed | tf_op | source)
XLA Modules:
  0.0 56.4 jit_solution(15206319943485670503)
XLA Ops:
  0.0 1.9 %collective-permute-start.2 = (bf16[576,128]{1,0:T(8,128)(2,1)}, bf16[576,128]{1,0:T(8,128)(2,1)S(1)}, u32[]{:S(2)}, u32[]{:S(2)}) collective-permute-start(bf16[576,128]{1,0:T(8,128)(2,1)} %bitcast.13), channel_id=1, source_target_pairs={{0,4},{4,16},{8,12},{12,24},{16,20},{20,32},{24,28},{28,40},{32,36... | collective-permute-start | bytes 442376 | tf_op jit(solution)/shard_map/ppermute | solution.py:199
  1.9 4.3 %collective-permute-start = (bf16[576,128]{1,0:T(8,128)(2,1)}, bf16[576,128]{1,0:T(8,128)(2,1)S(1)}, u32[]{:S(2)}, u32[]{:S(2)}) collective-permute-start(bf16[576,128]{1,0:T(8,128)(2,1)} %bitcast.14), channel_id=1, source_target_pairs={{0,8},{4,12},{8,16},{12,20},{16,24},{20,28},{24,32},{28,36},{32,40... | collective-permute-start | bytes 442376 | tf_op jit(solution)/shard_map/ppermute | solution.py:198
  6.2 0.0 copy-start.1
  6.2 0.0 copy-start.2
  6.2 3.5 %copy.6 = bf16[128,16,512]{0,2,1:T(8,128)(2,1)S(1)} copy(bf16[128,16,512]{2,1,0:T(8,128)(2,1)} %param.6) | data formatting | bytes 4194304 | tf_op args[2]
  9.8 0.0 copy-done.1
  9.8 0.0 copy-done.2
  9.8 0.0 copy-start
  9.8 0.5 own_grads.1
  10.3 7.7 %collective-permute-done.step_ref = bf16[576,128]{1,0:T(8,128)(2,1)S(1)} collective-permute-done((bf16[576,128]{1,0:T(8,128)(2,1)}, bf16[576,128]{1,0:T(8,128)(2,1)S(1)}, u32[]{:S(2)}, u32[]{:S(2)}) %collective-permute-start) | collective-permute-done | bytes 147488 | tf_op jit(solution)/shard_map/ppermute | solution.py:198
  18.0 1.9 %collective-permute-start.1 = (bf16[576,128]{1,0:T(8,128)(2,1)S(1)}, bf16[576,128]{1,0:T(8,128)(2,1)S(1)}, u32[]{:S(2)}, u32[]{:S(2)}) collective-permute-start(bf16[576,128]{1,0:T(8,128)(2,1)S(1)} %collective-permute-done.step_ref), channel_id=1, source_target_pairs={{0,4},{4,0},{8,12},{12,8},{16,20},{20,16},{24,28},{28,24},{32,36},... | collective-permute-start | bytes 442376 | tf_op jit(solution)/shard_map/ppermute | solution.py:204
  19.9 0.0 copy-done
  19.9 1.3 %products.1 = (f32[256,2048]{1,0:T(8,128)S(1)}, f32[128,2048]{1,0:T(8,128)S(1)}) custom-call(bf16[16,576,128]{2,1,0:T(8,128)(2,1)S(1)} %bitcast.10, bf16[16,512,128]{2,1,0:T(8,128)(2,1)S(1)} %bitcast.7, bf16[576,128]{1,0:T(8,128)(2,1)S(1)} %collective-permute-done.step_ref, bf16[576,128]{1,0:T(8,128)(2,1)S(1)} %bitcast.16), custom_call_target="tpu_custom_call" | custom-call | tf_op jit(solution)/shard_map/products/pallas_call | solution.py:94
  21.2 0.0 collective-permute-done.2.skip_ref
  21.2 0.0 collective-permute-done.1.swap_ref
  21.3 4.6 %first_grads.1 = (bf16[576,128]{1,0:T(8,128)(2,1)S(1)}, bf16[576,128]{1,0:T(8,128)(2,1)S(1)}, bf16[256,2048]{1,0:T(8,128)(2,1)S(1)}, bf16[256,2048]{1,0:T(8,128)(2,1)S(1)}) custom-call(s32[8,128]{1,0:T(8,128)S(1)} %get-tuple-element.16.seen_ref, bf16[16,576,128]{2,1,0:T(8,128)(2,1)S(1)} %bitcast.11, bf16[16,512,128]{2,1,0:T(8,128)(2,1)S(1)} %bitcast.8, ...), custom_call_target="tpu_custom_call" | custom-call | tf_op jit(solution)/shard_map/first_grads/pallas_call | solution.py:159
  25.8 2.4 %collective-permute-start.4 = (bf16[576,128]{1,0:T(8,128)(2,1)S(1)}, bf16[576,128]{1,0:T(8,128)(2,1)S(1)}, u32[]{:S(2)}, u32[]{:S(2)}) collective-permute-start(bf16[576,128]{1,0:T(8,128)(2,1)S(1)} %get-tuple-element.26), channel_id=1, source_target_pairs={{0,4},{4,0},{8,12},{12,8},{16,20},{20,16},{24,28},{28,24},{32,36},... | collective-permute-start | bytes 442376 | tf_op jit(solution)/shard_map/ppermute | solution.py:207
  28.2 4.5 %collective-permute-start.3 = (bf16[576,128]{1,0:T(8,128)(2,1)S(1)}, bf16[576,128]{1,0:T(8,128)(2,1)S(1)}, u32[]{:S(2)}, u32[]{:S(2)}) collective-permute-start(bf16[576,128]{1,0:T(8,128)(2,1)S(1)} %get-tuple-element.24), channel_id=1, source_target_pairs={{4,0},{16,4},{12,8},{24,12},{20,16},{32,20},{28,24},{40,28},{36,32... | collective-permute-start | bytes 442376 | tf_op jit(solution)/shard_map/ppermute | solution.py:208
  32.8 1.6 %second_grads.1 = (f32[576,128]{1,0:T(8,128)S(1)}, f32[576,128]{1,0:T(8,128)S(1)}) custom-call(bf16[16,576,128]{2,1,0:T(8,128)(2,1)S(1)} %bitcast.12, bf16[16,512,128]{2,1,0:T(8,128)(2,1)S(1)} %bitcast.9, bf16[256,2048]{1,0:T(8,128)(2,1)S(1)} %get-tuple-element.21.scores_ref, bf16[256,2048]{1,0:T(8,128)(2,1)S(1)} %get-tuple-element.22.low_ref), custom_call_target="tpu_custom_call" | custom-call | tf_op jit(solution)/shard_map/second_grads/pallas_call | solution.py:182
  34.4 0.0 collective-permute-done.4
  34.4 2.5 %collective-permute-start.5 = (bf16[576,128]{1,0:T(8,128)(2,1)S(1)}, bf16[576,128]{1,0:T(8,128)(2,1)S(1)}, u32[]{:S(2)}, u32[]{:S(2)}) collective-permute-start(bf16[576,128]{1,0:T(8,128)(2,1)S(1)} %add_convert_fusion.1), channel_id=1, source_target_pairs={{8,0},{12,4},{16,8},{20,12},{24,16},{28,20},{32,24},{36,28},{40,32... | collective-permute-start | bytes 442376 | tf_op jit(solution)/shard_map/ppermute | solution.py:211
  37.0 0.0 collective-permute-done.3
  37.0 5.1 %collective-permute-done.5 = bf16[576,128]{1,0:T(8,128)(2,1)S(1)} collective-permute-done((bf16[576,128]{1,0:T(8,128)(2,1)S(1)}, bf16[576,128]{1,0:T(8,128)(2,1)S(1)}, u32[]{:S(2)}, u32[]{:S(2)}) %collective-permute-start.5) | collective-permute-done | bytes 147488 | tf_op jit(solution)/shard_map/ppermute | solution.py:211
  42.0 0.1 add_convert_fusion
  42.1 0.1 broadcast_in_dim.2
  42.2 13.5 %all_to_all.5 = bf16[4,576,128]{2,1,0:T(8,128)(2,1)S(1)} all-to-all(bf16[4,576,128]{2,1,0:T(8,128)(2,1)S(1)} %broadcast_in_dim.2), channel_id=1, replica_groups=mesh['ctx'=128,'head'=4] {'head'}, dimensions={0} | all-to-all | bytes 1179648 | tf_op jit(solution)/shard_map/all_to_all | solution.py:215
  55.6 0.8 %convert_reduce_fusion = f32[576,128]{1,0:T(8,128)} fusion(bf16[4,576,128]{2,1,0:T(8,128)(2,1)S(1)} %all_to_all.5), kind=kLoop, calls=%fused_computation | loop fusion | flops 516096 | bytes 884736 | tf_op jit(solution)/shard_map/reduce_sum | solution.py:216
  (1 shorter events, 0.0 us)
Async XLA Ops:
  0.0 21.2 %collective-permute-start.2 = (bf16[576,128]{1,0:T(8,128)(2,1)}, bf16[576,128]{1,0:T(8,128)(2,1)S(1)}, u32[]{:S(2)}, u32[]{:S(2)}) collective-permute-start(bf16[576,128]{1,0:T(8,128)(2,1)} %bitcast.13), channel_id=1, source_target_pairs={{0,4},{4,16},{8,12},{12,24},{16,20},{20,32},{24,28},{28,40},{32,36... | collective-permute-start | bytes 442376 | tf_op jit(solution)/shard_map/ppermute | solution.py:199
  1.9 16.1 %collective-permute-start = (bf16[576,128]{1,0:T(8,128)(2,1)}, bf16[576,128]{1,0:T(8,128)(2,1)S(1)}, u32[]{:S(2)}, u32[]{:S(2)}) collective-permute-start(bf16[576,128]{1,0:T(8,128)(2,1)} %bitcast.14), channel_id=1, source_target_pairs={{0,8},{4,12},{8,16},{12,20},{16,24},{20,28},{24,32},{28,36},{32,40... | collective-permute-start | bytes 442376 | tf_op jit(solution)/shard_map/ppermute | solution.py:198
  6.2 3.6 %copy-start.1 = (bf16[128,576]{0,1:T(8,128)(2,1)S(1)}, bf16[128,576]{0,1:T(8,128)(2,1)}, u32[]{:S(2)}) copy-start(bf16[128,576]{0,1:T(8,128)(2,1)} %param.5) | copy-start | bytes 442372
  6.2 3.6 %copy-start.2 = (s32[64]{0:T(128)S(1)}, s32[64]{0:T(128)}, u32[]{:S(2)}) copy-start(s32[64]{0:T(128)} %param.7) | copy-start | bytes 772
  9.8 10.2 %copy-start = (bf16[128,16,576]{0,2,1:T(8,128)(2,1)S(1)}, bf16[128,16,576]{0,2,1:T(8,128)(2,1)}, u32[]{:S(2)}) copy-start(bf16[128,16,576]{0,2,1:T(8,128)(2,1)} %param.4) | copy-start | bytes 7077892
  18.0 3.3 %collective-permute-start.1 = (bf16[576,128]{1,0:T(8,128)(2,1)S(1)}, bf16[576,128]{1,0:T(8,128)(2,1)S(1)}, u32[]{:S(2)}, u32[]{:S(2)}) collective-permute-start(bf16[576,128]{1,0:T(8,128)(2,1)S(1)} %collective-permute-done.step_ref), channel_id=1, source_target_pairs={{0,4},{4,0},{8,12},{12,8},{16,20},{20,16},{24,28},{28,24},{32,36},... | collective-permute-start | bytes 442376 | tf_op jit(solution)/shard_map/ppermute | solution.py:204
  25.8 8.5 %collective-permute-start.4 = (bf16[576,128]{1,0:T(8,128)(2,1)S(1)}, bf16[576,128]{1,0:T(8,128)(2,1)S(1)}, u32[]{:S(2)}, u32[]{:S(2)}) collective-permute-start(bf16[576,128]{1,0:T(8,128)(2,1)S(1)} %get-tuple-element.26), channel_id=1, source_target_pairs={{0,4},{4,0},{8,12},{12,8},{16,20},{20,16},{24,28},{28,24},{32,36},... | collective-permute-start | bytes 442376 | tf_op jit(solution)/shard_map/ppermute | solution.py:207
  28.2 8.7 %collective-permute-start.3 = (bf16[576,128]{1,0:T(8,128)(2,1)S(1)}, bf16[576,128]{1,0:T(8,128)(2,1)S(1)}, u32[]{:S(2)}, u32[]{:S(2)}) collective-permute-start(bf16[576,128]{1,0:T(8,128)(2,1)S(1)} %get-tuple-element.24), channel_id=1, source_target_pairs={{4,0},{16,4},{12,8},{24,12},{20,16},{32,20},{28,24},{40,28},{36,32... | collective-permute-start | bytes 442376 | tf_op jit(solution)/shard_map/ppermute | solution.py:208
  34.4 7.6 %collective-permute-start.5 = (bf16[576,128]{1,0:T(8,128)(2,1)S(1)}, bf16[576,128]{1,0:T(8,128)(2,1)S(1)}, u32[]{:S(2)}, u32[]{:S(2)}) collective-permute-start(bf16[576,128]{1,0:T(8,128)(2,1)S(1)} %add_convert_fusion.1), channel_id=1, source_target_pairs={{8,0},{12,4},{16,8},{20,12},{24,16},{28,20},{32,24},{36,28},{40,32... | collective-permute-start | bytes 442376 | tf_op jit(solution)/shard_map/ppermute | solution.py:211

commit v3 on v2

--- a/solution.py
+++ b/solution.py
@@ -9,8 +9,9 @@
 
 BLOCK = 128
 GROUP = 8
+PART = 4
 LANES = 128
-OWN_FLOPS = 4 * 10 ** 9
+OWN_FLOPS = 1 * 10 ** 9
 
 softmax_scale = 192.0 ** (-0.5)
 to_exponent = softmax_scale * math.log2(math.e)
@@ -36,8 +37,8 @@
     return [(j, i) for i, j in pairs]
 
 
-def side_by_side(ref, at):
-    return jnp.concatenate([ref[at + h] for h in range(GROUP)], axis=1)
+def side_by_side(ref, at, count):
+    return jnp.concatenate([ref[at + h] for h in range(count)], axis=1)
 
 
 def own_kernel(shard_ref, docs_ref, g_ref, own_ref, seen_ref, grads_ref):
@@ -57,7 +58,7 @@
     rows = own_ref[:lat, :].T
     for at in range(0, heads, GROUP):
         grads_ref[:, at * blk:(at + GROUP) * blk] = jnp.dot(
-            rows, side_by_side(g_ref, at), preferred_element_type=jnp.float32)
+            rows, side_by_side(g_ref, at, GROUP), preferred_element_type=jnp.float32)
 
 
 def own_grads(shard, doc_blocks, g, own):
@@ -80,13 +81,13 @@
     rows = jnp.concatenate([step_ref[...].T, own_ref[...].T], axis=0)
     for at in range(0, heads, GROUP):
         where = slice(at * blk, (at + GROUP) * blk)
-        scores = jnp.dot(rows, side_by_side(q_ref, at), preferred_element_type=jnp.float32)
+        scores = jnp.dot(rows, side_by_side(q_ref, at, GROUP), preferred_element_type=jnp.float32)
         key = lax.broadcasted_iota(jnp.int32, scores[blk:].shape, 0)
         query = lax.broadcasted_iota(jnp.int32, scores[blk:].shape, 1) & (blk - 1)
         scores_ref[:blk, where] = scores[:blk]
         scores_ref[blk:, where] = jnp.where(key <= query, scores[blk:], -jnp.inf)
         grads_ref[:, where] = jnp.dot(
-            rows[:blk, :lat], side_by_side(g_ref, at), preferred_element_type=jnp.float32)
+            rows[:blk, :lat], side_by_side(g_ref, at, GROUP), preferred_element_type=jnp.float32)
 
 
 def products(q, g, step, own):
@@ -103,34 +104,20 @@
     )(q, g, step, own)
 
 
-def transposed_sums(q, g, grad_scores, low):
-    lat = g.shape[0]
-    upper = lax.dot_general(
-        jnp.concatenate([q[:lat], g], axis=1), jnp.concatenate([grad_scores, low], axis=1),
-        NT, preferred_element_type=jnp.float32)
-    lower = lax.dot_general(q[lat:], grad_scores, NT, preferred_element_type=jnp.float32)
-    return upper, lower
-
-
-def put(refs, upper, lower):
-    lat = upper.shape[0]
-    for j, ref in enumerate(refs):
-        blk = ref.shape[1]
-        ref[:lat, :] = upper[:, j * blk:(j + 1) * blk].astype(ref.dtype)
-        ref[lat:, :] = lower[:, j * blk:(j + 1) * blk].astype(ref.dtype)
-
-
 def first_kernel(seen_ref, q_ref, g_ref, swap_ref, skip_ref, near_s, step_g, own_g,
-                 swap_out, skip_out, scores_out, low_out):
+                 swap_out, skip_out, step_out, own_out):
     heads, lat, blk = g_ref.shape
     rows = jnp.concatenate([swap_ref[...].T, skip_ref[...].T], axis=0)
-    upper = lower = None
-    for at in range(0, heads, GROUP):
-        where = pl.ds(at * blk, GROUP * blk)
-        q = side_by_side(q_ref, at)
-        g = side_by_side(g_ref, at)
+
+    def products_of(at):
+        q = side_by_side(q_ref, at, PART)
+        g = side_by_side(g_ref, at, PART)
         scores = jnp.dot(rows, q, preferred_element_type=jnp.float32)
         grad_probs = jnp.dot(rows[:, :lat], g, preferred_element_type=jnp.float32)
+        return at, q, g, scores, grad_probs
+
+    def sums_of(at, q, g, scores, grad_probs):
+        where = slice(at * blk, (at + PART) * blk)
         grad_probs = jnp.concatenate([grad_probs, step_g[:, where], own_g[:, where]], axis=0)
         parts = [scores[:blk], scores[blk:], near_s[:blk, where], near_s[blk:, where]]
         tops = [jnp.max(part, axis=0, keepdims=True) for part in parts]
@@ -144,47 +131,35 @@
         dot = jnp.sum(raised * grad_probs, axis=0, keepdims=True) * inverse
         low = (raised * inverse).astype(jnp.bfloat16)
         grad_scores = ((raised * (inverse * softmax_scale)) * (grad_probs - dot)).astype(jnp.bfloat16)
-        scores_out[:, where] = grad_scores[2 * blk:]
-        low_out[:, where] = low[2 * blk:]
-        up, down = transposed_sums(q, g, grad_scores[:2 * blk], low[:2 * blk])
-        upper = up if upper is None else upper + up
-        lower = down if lower is None else lower + down
-    put((swap_out, skip_out), upper, lower)
+        value = lax.dot_general(g, low, NT, preferred_element_type=jnp.float32)
+        key = lax.dot_general(q, grad_scores, NT, preferred_element_type=jnp.float32)
+        return value, key
+
+    value = key = None
+    after_this = products_of(0)
+    for at in range(0, heads, PART):
+        this = after_this
+        if at + PART < heads:
+            after_this = products_of(at + PART)
+        more_value, more_key = sums_of(*this)
+        value = more_value if value is None else value + more_value
+        key = more_key if key is None else key + more_key
+    for j, ref in enumerate((swap_out, skip_out, step_out, own_out)):
+        mine = slice(j * blk, (j + 1) * blk)
+        ref[:lat, :] = (key[:lat, mine] + value[:, mine]).astype(ref.dtype)
+        ref[lat:, :] = key[lat:, mine].astype(ref.dtype)
 
 
 def first_grads(seen, q, g, swap, skip, near_scores, step_grads, own_grads):
     heads, width, rows = q.shape
     sent = jax.ShapeDtypeStruct((width, rows), jnp.bfloat16)
-    kept = jax.ShapeDtypeStruct((2 * rows, heads * rows), jnp.bfloat16)
+    kept = jax.ShapeDtypeStruct((width, rows), jnp.float32)
     return pl.pallas_call(
         first_kernel,
         in_specs=[VMEM] * 8, out_specs=[VMEM] * 4, out_shape=[sent, sent, kept, kept],
         compiler_params=pltpu.CompilerParams(vmem_limit_bytes=30 * 1024 * 1024),
         name="first_grads",
     )(seen, q, g, swap, skip, near_scores, step_grads, own_grads)
-
-
-def second_kernel(q_ref, g_ref, scores_ref, low_ref, step_out, own_out):
-    heads, lat, blk = g_ref.shape
-    upper = lower = None
-    for at in range(0, heads, GROUP):
-        where = pl.ds(at * blk, GROUP * blk)
-        up, down = transposed_sums(
-            side_by_side(q_ref, at), side_by_side(g_ref, at), scores_ref[:, where], low_ref[:, where])
-        upper = up if upper is None else upper + up
-        lower = down if lower is None else lower + down
-    put((step_out, own_out), upper, lower)
-
-
-def second_grads(q, g, grad_scores, low):
-    heads, width, rows = q.shape
-    made = jax.ShapeDtypeStruct((width, rows), jnp.float32)
-    return pl.pallas_call(
-        second_kernel,
-        in_specs=[VMEM] * 4, out_specs=[VMEM] * 2, out_shape=[made, made],
-        compiler_params=pltpu.CompilerParams(vmem_limit_bytes=30 * 1024 * 1024),
-        name="second_grads",
-    )(q, g, grad_scores, low)
 
 
 def after(x, *others):
@@ -203,10 +178,9 @@
     step = after(step, of_own)
     swap = lax.ppermute(step, "ctx", swap_pairs(n))
     near_scores, of_step = products(q, g, step, own)
-    swap, skip, grad_scores, low = first_grads(seen, q, g, swap, skip, near_scores, of_step, of_own)
+    swap, skip, step, near = first_grads(seen, q, g, swap, skip, near_scores, of_step, of_own)
     swap = lax.ppermute(swap, "ctx", swap_pairs(n))
     skip = lax.ppermute(skip, "ctx", turned(skip_pairs(n)))
-    step, near = second_grads(q, g, grad_scores, low)
     step = (step + swap.astype(jnp.float32)).astype(jnp.bfloat16)
     step = lax.ppermute(step, "ctx", turned(step_pairs(n)))
     low = (near + skip.astype(jnp.float32) + step.astype(jnp.float32)).astype(jnp.bfloat16)

time: 56.8 us -> 55.4 us (0.975)
  the two profiles are of different devices: /device:TPU:24 before, /device:TPU:40 now
where the time goes in v3:
time: 55.4 us; the launch traced here: 55 us
  starting transfers between devices  17.4 us (31%)
  blocking collectives  13.7 us (25%)
  waiting for transfers between devices  13 us (23%)
  Pallas kernels  6.19 us (11%)
  local copies, waits for them, and re-layouts  3.62 us (7%)
  other arithmetic  0.9 us (2%)
    all_to_all x1, blocking collectives, shards(): parts = lax.all_to_all(spread, 'head', 0, 0, tiled=True)  13.7 us
    ppermute x1, waiting for transfers between devices, shards(): step = lax.ppermute(own, 'ctx', step_pairs(n))  7.1 us
    ppermute x1, waiting for transfers between devices, shards(): step = lax.ppermute(step, 'ctx', turned(step_pairs(n)))  5.84 us
    pallas_call x1, Pallas kernels, first_grads(): pl.pallas_call(first_kernel, in_specs=[VMEM] * 8, out_specs=[VMEM] * 4, o...  4.43 us
    ppermute x1, starting transfers between devices, shards(): step = lax.ppermute(own, 'ctx', step_pairs(n))  4.27 us
    ppermute x1, starting transfers between devices, shards(): skip = lax.ppermute(skip, 'ctx', turned(skip_pairs(n)))  3.66 us
    unnamed x7, local copies, waits for them, and re-layouts  3.54 us
    ppermute x1, starting transfers between devices, shards(): step = lax.ppermute(step, 'ctx', turned(step_pairs(n)))  3.29 us
  transfers between devices with their start and end apart: 6, of which 2 were waited for; matrix products, arithmetic and copies ran while one was open for 6% of the time, Pallas kernels for 3%

profile of v3, /device:TPU:40, one launch (start us, length us, event | category | flops | bytes accessed | tf_op | source)
XLA Modules:
  0.0 55.0 jit_solution(18279742544135874838)
XLA Ops:
  0.0 4.3 %collective-permute-start = (bf16[576,128]{1,0:T(8,128)(2,1)}, bf16[576,128]{1,0:T(8,128)(2,1)S(1)}, u32[]{:S(2)}, u32[]{:S(2)}) collective-permute-start(bf16[576,128]{1,0:T(8,128)(2,1)} %bitcast.11), channel_id=1, source_target_pairs={{0,8},{4,12},{8,16},{12,20},{16,24},{20,28},{24,32},{28,36},{32,40... | collective-permute-start | bytes 442376 | tf_op jit(solution)/shard_map/ppermute | solution.py:173
  4.3 1.9 %collective-permute-start.2 = (bf16[576,128]{1,0:T(8,128)(2,1)}, bf16[576,128]{1,0:T(8,128)(2,1)S(1)}, u32[]{:S(2)}, u32[]{:S(2)}) collective-permute-start(bf16[576,128]{1,0:T(8,128)(2,1)} %bitcast.12), channel_id=1, source_target_pairs={{0,4},{4,16},{8,12},{12,24},{16,20},{20,32},{24,28},{28,40},{32,36... | collective-permute-start | bytes 442376 | tf_op jit(solution)/shard_map/ppermute | solution.py:174
  6.2 0.0 copy-start.1
  6.2 0.0 copy-start.2
  6.2 3.5 %copy.6 = bf16[128,16,512]{0,2,1:T(8,128)(2,1)S(1)} copy(bf16[128,16,512]{2,1,0:T(8,128)(2,1)} %param.6) | data formatting | bytes 4194304 | tf_op args[2]
  9.8 0.0 copy-start
  9.8 0.0 copy-done.1
  9.8 0.0 copy-done.2
  9.8 0.5 own_grads.1
  10.3 7.1 %collective-permute-done.step_ref = bf16[576,128]{1,0:T(8,128)(2,1)S(1)} collective-permute-done((bf16[576,128]{1,0:T(8,128)(2,1)}, bf16[576,128]{1,0:T(8,128)(2,1)S(1)}, u32[]{:S(2)}, u32[]{:S(2)}) %collective-permute-start) | collective-permute-done | bytes 147488 | tf_op jit(solution)/shard_map/ppermute | solution.py:173
  17.4 1.9 %collective-permute-start.1 = (bf16[576,128]{1,0:T(8,128)(2,1)S(1)}, bf16[576,128]{1,0:T(8,128)(2,1)S(1)}, u32[]{:S(2)}, u32[]{:S(2)}) collective-permute-start(bf16[576,128]{1,0:T(8,128)(2,1)S(1)} %collective-permute-done.step_ref), channel_id=1, source_target_pairs={{0,4},{4,0},{8,12},{12,8},{16,20},{20,16},{24,28},{28,24},{32,36},... | collective-permute-start | bytes 442376 | tf_op jit(solution)/shard_map/ppermute | solution.py:179
  19.3 0.0 copy-done
  19.3 1.3 %products.1 = (f32[256,2048]{1,0:T(8,128)S(1)}, f32[128,2048]{1,0:T(8,128)S(1)}) custom-call(bf16[16,576,128]{2,1,0:T(8,128)(2,1)S(1)} %bitcast.9, bf16[16,512,128]{2,1,0:T(8,128)(2,1)S(1)} %bitcast.7, bf16[576,128]{1,0:T(8,128)(2,1)S(1)} %collective-permute-done.step_ref, bf16[576,128]{1,0:T(8,128)(2,1)S(1)} %bitcast.14), custom_call_target="tpu_custom_call" | custom-call | tf_op jit(solution)/shard_map/products/pallas_call | solution.py:95
  20.6 0.0 collective-permute-done.2.skip_ref
  20.6 0.0 collective-permute-done.1.swap_ref
  20.6 4.4 %first_grads.1 = (bf16[576,128]{1,0:T(8,128)(2,1)S(1)}, bf16[576,128]{1,0:T(8,128)(2,1)S(1)}, f32[576,128]{1,0:T(8,128)S(1)}, f32[576,128]{1,0:T(8,128)S(1)}) custom-call(s32[8,128]{1,0:T(8,128)S(1)} %get-tuple-element.14.seen_ref, bf16[16,576,128]{2,1,0:T(8,128)(2,1)S(1)} %bitcast.10, bf16[16,512,128]{2,1,0:T(8,128)(2,1)S(1)} %bitcast.8, ...), custom_call_target="tpu_custom_call" | custom-call | tf_op jit(solution)/shard_map/first_grads/pallas_call | solution.py:157
  25.1 2.4 %collective-permute-start.4 = (bf16[576,128]{1,0:T(8,128)(2,1)S(1)}, bf16[576,128]{1,0:T(8,128)(2,1)S(1)}, u32[]{:S(2)}, u32[]{:S(2)}) collective-permute-start(bf16[576,128]{1,0:T(8,128)(2,1)S(1)} %get-tuple-element.22), channel_id=1, source_target_pairs={{0,4},{4,0},{8,12},{12,8},{16,20},{20,16},{24,28},{28,24},{32,36},... | collective-permute-start | bytes 442376 | tf_op jit(solution)/shard_map/ppermute | solution.py:182
  27.5 3.7 %collective-permute-start.3 = (bf16[576,128]{1,0:T(8,128)(2,1)S(1)}, bf16[576,128]{1,0:T(8,128)(2,1)S(1)}, u32[]{:S(2)}, u32[]{:S(2)}) collective-permute-start(bf16[576,128]{1,0:T(8,128)(2,1)S(1)} %get-tuple-element.20), channel_id=1, source_target_pairs={{4,0},{16,4},{12,8},{24,12},{20,16},{32,20},{28,24},{40,28},{36,32... | collective-permute-start | bytes 442376 | tf_op jit(solution)/shard_map/ppermute | solution.py:183
  31.1 0.0 collective-permute-done.4
  31.2 3.3 %collective-permute-start.5 = (bf16[576,128]{1,0:T(8,128)(2,1)S(1)}, bf16[576,128]{1,0:T(8,128)(2,1)S(1)}, u32[]{:S(2)}, u32[]{:S(2)}) collective-permute-start(bf16[576,128]{1,0:T(8,128)(2,1)S(1)} %add_convert_fusion.1), channel_id=1, source_target_pairs={{8,0},{12,4},{16,8},{20,12},{24,16},{28,20},{32,24},{36,28},{40,32... | collective-permute-start | bytes 442376 | tf_op jit(solution)/shard_map/ppermute | solution.py:185
  34.5 0.0 collective-permute-done.3
  34.5 5.8 %collective-permute-done.5 = bf16[576,128]{1,0:T(8,128)(2,1)S(1)} collective-permute-done((bf16[576,128]{1,0:T(8,128)(2,1)S(1)}, bf16[576,128]{1,0:T(8,128)(2,1)S(1)}, u32[]{:S(2)}, u32[]{:S(2)}) %collective-permute-start.5) | collective-permute-done | bytes 147488 | tf_op jit(solution)/shard_map/ppermute | solution.py:185
  40.3 0.1 add_convert_fusion
  40.4 0.1 broadcast_in_dim.2
  40.5 13.7 %all_to_all.5 = bf16[4,576,128]{2,1,0:T(8,128)(2,1)S(1)} all-to-all(bf16[4,576,128]{2,1,0:T(8,128)(2,1)S(1)} %broadcast_in_dim.2), channel_id=1, replica_groups=mesh['ctx'=128,'head'=4] {'head'}, dimensions={0} | all-to-all | bytes 1179648 | tf_op jit(solution)/shard_map/all_to_all | solution.py:189
  54.2 0.8 %convert_reduce_fusion = f32[576,128]{1,0:T(8,128)} fusion(bf16[4,576,128]{2,1,0:T(8,128)(2,1)S(1)} %all_to_all.5), kind=kLoop, calls=%fused_computation | loop fusion | flops 516096 | bytes 884736 | tf_op jit(solution)/shard_map/reduce_sum | solution.py:190
  (1 shorter events, 0.0 us)
Async XLA Ops:
  0.0 17.4 %collective-permute-start = (bf16[576,128]{1,0:T(8,128)(2,1)}, bf16[576,128]{1,0:T(8,128)(2,1)S(1)}, u32[]{:S(2)}, u32[]{:S(2)}) collective-permute-start(bf16[576,128]{1,0:T(8,128)(2,1)} %bitcast.11), channel_id=1, source_target_pairs={{0,8},{4,12},{8,16},{12,20},{16,24},{20,28},{24,32},{28,36},{32,40... | collective-permute-start | bytes 442376 | tf_op jit(solution)/shard_map/ppermute | solution.py:173
  4.3 16.3 %collective-permute-start.2 = (bf16[576,128]{1,0:T(8,128)(2,1)}, bf16[576,128]{1,0:T(8,128)(2,1)S(1)}, u32[]{:S(2)}, u32[]{:S(2)}) collective-permute-start(bf16[576,128]{1,0:T(8,128)(2,1)} %bitcast.12), channel_id=1, source_target_pairs={{0,4},{4,16},{8,12},{12,24},{16,20},{20,32},{24,28},{28,40},{32,36... | collective-permute-start | bytes 442376 | tf_op jit(solution)/shard_map/ppermute | solution.py:174
  6.2 3.6 %copy-start.1 = (bf16[128,576]{0,1:T(8,128)(2,1)S(1)}, bf16[128,576]{0,1:T(8,128)(2,1)}, u32[]{:S(2)}) copy-start(bf16[128,576]{0,1:T(8,128)(2,1)} %param.5) | copy-start | bytes 442372
  6.2 3.6 %copy-start.2 = (s32[64]{0:T(128)S(1)}, s32[64]{0:T(128)}, u32[]{:S(2)}) copy-start(s32[64]{0:T(128)} %param.7) | copy-start | bytes 772
  9.8 9.5 %copy-start = (bf16[128,16,576]{0,2,1:T(8,128)(2,1)S(1)}, bf16[128,16,576]{0,2,1:T(8,128)(2,1)}, u32[]{:S(2)}) copy-start(bf16[128,16,576]{0,2,1:T(8,128)(2,1)} %param.4) | copy-start | bytes 7077892
  17.4 3.3 %collective-permute-start.1 = (bf16[576,128]{1,0:T(8,128)(2,1)S(1)}, bf16[576,128]{1,0:T(8,128)(2,1)S(1)}, u32[]{:S(2)}, u32[]{:S(2)}) collective-permute-start(bf16[576,128]{1,0:T(8,128)(2,1)S(1)} %collective-permute-done.step_ref), channel_id=1, source_target_pairs={{0,4},{4,0},{8,12},{12,8},{16,20},{20,16},{24,28},{28,24},{32,36},... | collective-permute-start | bytes 442376 | tf_op jit(solution)/shard_map/ppermute | solution.py:179
  25.1 6.1 %collective-permute-start.4 = (bf16[576,128]{1,0:T(8,128)(2,1)S(1)}, bf16[576,128]{1,0:T(8,128)(2,1)S(1)}, u32[]{:S(2)}, u32[]{:S(2)}) collective-permute-start(bf16[576,128]{1,0:T(8,128)(2,1)S(1)} %get-tuple-element.22), channel_id=1, source_target_pairs={{0,4},{4,0},{8,12},{12,8},{16,20},{20,16},{24,28},{28,24},{32,36},... | collective-permute-start | bytes 442376 | tf_op jit(solution)/shard_map/ppermute | solution.py:182
  27.5 7.0 %collective-permute-start.3 = (bf16[576,128]{1,0:T(8,128)(2,1)S(1)}, bf16[576,128]{1,0:T(8,128)(2,1)S(1)}, u32[]{:S(2)}, u32[]{:S(2)}) collective-permute-start(bf16[576,128]{1,0:T(8,128)(2,1)S(1)} %get-tuple-element.20), channel_id=1, source_target_pairs={{4,0},{16,4},{12,8},{24,12},{20,16},{32,20},{28,24},{40,28},{36,32... | collective-permute-start | bytes 442376 | tf_op jit(solution)/shard_map/ppermute | solution.py:183
  31.2 9.1 %collective-permute-start.5 = (bf16[576,128]{1,0:T(8,128)(2,1)S(1)}, bf16[576,128]{1,0:T(8,128)(2,1)S(1)}, u32[]{:S(2)}, u32[]{:S(2)}) collective-permute-start(bf16[576,128]{1,0:T(8,128)(2,1)S(1)} %add_convert_fusion.1), channel_id=1, source_target_pairs={{8,0},{12,4},{16,8},{20,12},{24,16},{28,20},{32,24},{36,28},{40,32... | collective-permute-start | bytes 442376 | tf_op jit(solution)/shard_map/ppermute | solution.py:185

commit v4 on v3

--- a/solution.py
+++ b/solution.py
@@ -166,6 +166,11 @@
     return lax.optimization_barrier((x,) + others)[0]
 
 
+def from_partner(x, n, shard):
+    both = lax.all_gather(x, "ctx", axis_index_groups=[[i, i + 1] for i in range(0, n, 2)])
+    return jnp.where(shard % 2 == 0, both[1], both[0])
+
+
 def shards(queries, latent, out_grad, doc_blocks):
     n = lax.axis_size("ctx")
     shard = lax.axis_index("ctx")
@@ -176,17 +181,19 @@
     g = jnp.transpose(out_grad, (1, 2, 0))
     seen, of_own = own_grads(shard.reshape(1), doc_blocks.reshape(1, -1), g, own)
     step = after(step, of_own)
-    swap = lax.ppermute(step, "ctx", swap_pairs(n))
+    swap = from_partner(step, n, shard)
     near_scores, of_step = products(q, g, step, own)
     swap, skip, step, near = first_grads(seen, q, g, swap, skip, near_scores, of_step, of_own)
-    swap = lax.ppermute(swap, "ctx", swap_pairs(n))
+    swap = from_partner(swap, n, shard)
+    step = (step + swap.astype(jnp.float32)).astype(jnp.bfloat16)
+    skip = after(skip, step)
+    step = lax.ppermute(step, "ctx", turned(step_pairs(n)))
     skip = lax.ppermute(skip, "ctx", turned(skip_pairs(n)))
-    step = (step + swap.astype(jnp.float32)).astype(jnp.bfloat16)
-    step = lax.ppermute(step, "ctx", turned(step_pairs(n)))
-    low = (near + skip.astype(jnp.float32) + step.astype(jnp.float32)).astype(jnp.bfloat16)
-    heads = lax.axis_size("head")
-    spread = jnp.broadcast_to(low[None], (heads,) + low.shape)
-    parts = lax.all_to_all(spread, "head", 0, 0, tiled=True)
+    near = near + step.astype(jnp.float32)
+    near, skip = lax.optimization_barrier((near, skip))
+    low = (near + skip.astype(jnp.float32)).astype(jnp.bfloat16)
+    low = jnp.sum(lax.all_gather(low, "head", axis_index_groups=[[0, 1], [2, 3]]).astype(jnp.float32), axis=0)
+    parts = lax.all_gather(low.astype(jnp.bfloat16), "head", axis_index_groups=[[0, 3], [1, 2]])
     return jnp.sum(parts.astype(jnp.float32), axis=0).T
 
 

time: 55.4 us -> 53.5 us (0.966)
  the two profiles are of different devices: /device:TPU:40 before, /device:TPU:57 now
where the time goes in v4:
time: 53.5 us; the launch traced here: 53.2 us
  blocking collectives  19.3 us (36%)
  starting transfers between devices  17.9 us (33%)
  Pallas kernels  6.19 us (12%)
  waiting for transfers between devices  5.26 us (10%)
  local copies, waits for them, and re-layouts  3.54 us (7%)
  other arithmetic  0.94 us (2%)
    all_gather x1, blocking collectives, shards(): lax.all_gather(low.astype(jnp.bfloat16), 'head', axis_index_groups=[[0, 3...  7.55 us
    ppermute x1, starting transfers between devices, shards(): skip = lax.ppermute(own, 'ctx', skip_pairs(n))  6.65 us
    all_gather x2, blocking collectives, from_partner(): lax.all_gather(x, 'ctx', axis_index_groups=[[i, i + 1] for i in range(0,...  6.41 us
    all_gather x1, blocking collectives, shards(): lax.all_gather(low, 'head', axis_index_groups=[[0, 1], [2, 3]])  5.29 us
    ppermute x1, starting transfers between devices, shards(): step = lax.ppermute(step, 'ctx', turned(step_pairs(n)))  4.7 us
    ppermute x1, waiting for transfers between devices, shards(): skip = lax.ppermute(skip, 'ctx', turned(skip_pairs(n)))  4.48 us
    pallas_call x1, Pallas kernels, first_grads(): pl.pallas_call(first_kernel, in_specs=[VMEM] * 8, out_specs=[VMEM] * 4, o...  4.44 us
    ppermute x1, starting transfers between devices, shards(): step = lax.ppermute(own, 'ctx', step_pairs(n))  3.99 us
  transfers between devices with their start and end apart: 4, of which 3 were waited for; matrix products, arithmetic and copies ran while one was open for 7% of the time, Pallas kernels for 3%

profile of v4, /device:TPU:57, one launch (start us, length us, event | category | flops | bytes accessed | tf_op | source)
XLA Modules:
  0.0 53.2 jit_solution(12127799293972703257)
XLA Ops:
  0.0 4.0 %collective-permute-start = (bf16[576,128]{1,0:T(8,128)(2,1)}, bf16[576,128]{1,0:T(8,128)(2,1)S(1)}, u32[]{:S(2)}, u32[]{:S(2)}) collective-permute-start(bf16[576,128]{1,0:T(8,128)(2,1)} %bitcast.14), channel_id=1, source_target_pairs={{0,8},{4,12},{8,16},{12,20},{16,24},{20,28},{24,32},{28,36},{32,40... | collective-permute-start | bytes 442376 | tf_op jit(solution)/shard_map/ppermute | solution.py:178
  4.0 6.6 %collective-permute-start.1 = (bf16[576,128]{1,0:T(8,128)(2,1)}, bf16[576,128]{1,0:T(8,128)(2,1)S(1)}, u32[]{:S(2)}, u32[]{:S(2)}) collective-permute-start(bf16[576,128]{1,0:T(8,128)(2,1)} %bitcast.15), channel_id=1, source_target_pairs={{0,4},{4,16},{8,12},{12,24},{16,20},{20,32},{24,28},{28,40},{32,36... | collective-permute-start | bytes 442376 | tf_op jit(solution)/shard_map/ppermute | solution.py:179
  10.7 0.0 copy-start.1
  10.7 0.0 copy-start.2
  10.7 3.5 %copy.6 = bf16[128,16,512]{0,2,1:T(8,128)(2,1)S(1)} copy(bf16[128,16,512]{2,1,0:T(8,128)(2,1)} %param.6) | data formatting | bytes 4194304 | tf_op args[2]
  14.2 0.0 copy-start
  14.2 0.0 copy-done.1
  14.2 0.0 copy-done.2
  14.3 0.5 own_grads.1
  14.7 0.5 collective-permute-done.step_ref
  15.2 4.4 %all-gather = bf16[1152,128]{1,0:T(8,128)(2,1)S(1)} all-gather(bf16[576,128]{1,0:T(8,128)(2,1)S(1)} %collective-permute-done.step_ref), channel_id=2, replica_groups={{0,4},{8,12},{16,20},{24,28},{32,36},{40,44},{48,52},{56,60},{64,68},{7..., dimensions={0}, use_global_device_ids=true | all-gather | bytes 442368 | tf_op jit(solution)/shard_map/all_gather | solution.py:170
  19.6 0.0 copy-done
  19.6 1.3 %products.1 = (f32[256,2048]{1,0:T(8,128)S(1)}, f32[128,2048]{1,0:T(8,128)S(1)}) custom-call(bf16[16,576,128]{2,1,0:T(8,128)(2,1)S(1)} %bitcast.12, bf16[16,512,128]{2,1,0:T(8,128)(2,1)S(1)} %bitcast.10, bf16[576,128]{1,0:T(8,128)(2,1)S(1)} %collective-permute-done.step_ref, bf16[576,128]{1,0:T(8,128)(2,1)S(1)} %bitcast.17), custom_call_target="tpu_custom_call" | custom-call | tf_op jit(solution)/shard_map/products/pallas_call | solution.py:95
  20.9 0.0 collective-permute-done.1.skip_ref
  20.9 4.4 %first_grads.1 = (bf16[576,128]{1,0:T(8,128)(2,1)S(1)}, bf16[576,128]{1,0:T(8,128)(2,1)S(1)}, f32[576,128]{1,0:T(8,128)S(1)}, f32[576,128]{1,0:T(8,128)S(1)}) custom-call(s32[8,128]{1,0:T(8,128)S(1)} %get-tuple-element.17.seen_ref, bf16[16,576,128]{2,1,0:T(8,128)(2,1)S(1)} %bitcast.13, bf16[16,512,128]{2,1,0:T(8,128)(2,1)S(1)} %bitcast.11, ...), custom_call_target="tpu_custom_call" | custom-call | tf_op jit(solution)/shard_map/first_grads/pallas_call | solution.py:157
  25.4 2.0 %all-gather.1 = bf16[1152,128]{1,0:T(8,128)(2,1)S(1)} all-gather(bf16[576,128]{1,0:T(8,128)(2,1)S(1)} %get-tuple-element.24), channel_id=3, replica_groups={{0,4},{8,12},{16,20},{24,28},{32,36},{40,44},{48,52},{56,60},{64,68},{7..., dimensions={0}, use_global_device_ids=true | all-gather | bytes 442368 | tf_op jit(solution)/shard_map/all_gather | solution.py:170
  27.4 0.1 fusion
  27.5 4.7 %collective-permute-start.2 = (bf16[576,128]{1,0:T(8,128)(2,1)S(1)}, bf16[576,128]{1,0:T(8,128)(2,1)S(1)}, u32[]{:S(2)}, u32[]{:S(2)}) collective-permute-start(bf16[576,128]{1,0:T(8,128)(2,1)S(1)} %fusion), channel_id=1, source_target_pairs={{8,0},{12,4},{16,8},{20,12},{24,16},{28,20},{32,24},{36,28},{40,32... | collective-permute-start | bytes 442376 | tf_op jit(solution)/shard_map/ppermute | solution.py:190
  32.2 2.6 %collective-permute-start.3 = (bf16[576,128]{1,0:T(8,128)(2,1)S(1)}, bf16[576,128]{1,0:T(8,128)(2,1)S(1)}, u32[]{:S(2)}, u32[]{:S(2)}) collective-permute-start(bf16[576,128]{1,0:T(8,128)(2,1)S(1)} %get-tuple-element.26), channel_id=1, source_target_pairs={{4,0},{16,4},{12,8},{24,12},{20,16},{32,20},{28,24},{40,28},{36,32... | collective-permute-start | bytes 442376 | tf_op jit(solution)/shard_map/ppermute | solution.py:191
  34.7 0.3 collective-permute-done.2
  35.0 4.5 %collective-permute-done.3 = bf16[576,128]{1,0:T(8,128)(2,1)S(1)} collective-permute-done((bf16[576,128]{1,0:T(8,128)(2,1)S(1)}, bf16[576,128]{1,0:T(8,128)(2,1)S(1)}, u32[]{:S(2)}, u32[]{:S(2)}) %collective-permute-start.3) | collective-permute-done | bytes 147488 | tf_op jit(solution)/shard_map/ppermute | solution.py:191
  39.6 5.3 %all-gather.2 = bf16[1152,128]{1,0:T(8,128)(2,1)S(1)} all-gather(bf16[576,128]{1,0:T(8,128)(2,1)S(1)} %add_convert_fusion), channel_id=4, replica_groups={{0,1},{2,3},{4,5},{6,7},{8,9},{10,11},{12,13},{14,15},{16,17},{18,19},{..., dimensions={0}, use_global_device_ids=true | all-gather | bytes 442368 | tf_op jit(solution)/shard_map/all_gather | solution.py:195
  44.9 0.1 reduce_sum.21
  44.9 7.6 %all-gather.3 = bf16[1152,128]{1,0:T(8,128)(2,1)S(1)} all-gather(bf16[576,128]{1,0:T(8,128)(2,1)S(1)} %reduce_sum.21), channel_id=5, replica_groups={{0,3},{1,2},{4,7},{5,6},{8,11},{9,10},{12,15},{13,14},{16,19},{17,18},{..., dimensions={0}, use_global_device_ids=true | all-gather | bytes 442368 | tf_op jit(solution)/shard_map/all_gather | solution.py:196
  52.5 0.8 %convert_reduce_fusion = f32[576,128]{1,0:T(8,128)} fusion(bf16[2,576,128]{2,1,0:T(8,128)(2,1)S(1)} %bitcast.20), kind=kLoop, calls=%fused_computation | loop fusion | flops 221184 | bytes 589824 | tf_op jit(solution)/shard_map/reduce_sum | solution.py:197
  (3 shorter events, 0.1 us)
Async XLA Ops:
  0.0 15.2 %collective-permute-start = (bf16[576,128]{1,0:T(8,128)(2,1)}, bf16[576,128]{1,0:T(8,128)(2,1)S(1)}, u32[]{:S(2)}, u32[]{:S(2)}) collective-permute-start(bf16[576,128]{1,0:T(8,128)(2,1)} %bitcast.14), channel_id=1, source_target_pairs={{0,8},{4,12},{8,16},{12,20},{16,24},{20,28},{24,32},{28,36},{32,40... | collective-permute-start | bytes 442376 | tf_op jit(solution)/shard_map/ppermute | solution.py:178
  4.0 16.9 %collective-permute-start.1 = (bf16[576,128]{1,0:T(8,128)(2,1)}, bf16[576,128]{1,0:T(8,128)(2,1)S(1)}, u32[]{:S(2)}, u32[]{:S(2)}) collective-permute-start(bf16[576,128]{1,0:T(8,128)(2,1)} %bitcast.15), channel_id=1, source_target_pairs={{0,4},{4,16},{8,12},{12,24},{16,20},{20,32},{24,28},{28,40},{32,36... | collective-permute-start | bytes 442376 | tf_op jit(solution)/shard_map/ppermute | solution.py:179
  10.7 3.6 %copy-start.1 = (bf16[128,576]{0,1:T(8,128)(2,1)S(1)}, bf16[128,576]{0,1:T(8,128)(2,1)}, u32[]{:S(2)}) copy-start(bf16[128,576]{0,1:T(8,128)(2,1)} %param.5) | copy-start | bytes 442372
  10.7 3.6 %copy-start.2 = (s32[64]{0:T(128)S(1)}, s32[64]{0:T(128)}, u32[]{:S(2)}) copy-start(s32[64]{0:T(128)} %param.7) | copy-start | bytes 772
  14.2 5.4 %copy-start = (bf16[128,16,576]{0,2,1:T(8,128)(2,1)S(1)}, bf16[128,16,576]{0,2,1:T(8,128)(2,1)}, u32[]{:S(2)}) copy-start(bf16[128,16,576]{0,2,1:T(8,128)(2,1)} %param.4) | copy-start | bytes 7077892
  27.5 7.6 %collective-permute-start.2 = (bf16[576,128]{1,0:T(8,128)(2,1)S(1)}, bf16[576,128]{1,0:T(8,128)(2,1)S(1)}, u32[]{:S(2)}, u32[]{:S(2)}) collective-permute-start(bf16[576,128]{1,0:T(8,128)(2,1)S(1)} %fusion), channel_id=1, source_target_pairs={{8,0},{12,4},{16,8},{20,12},{24,16},{28,20},{32,24},{36,28},{40,32... | collective-permute-start | bytes 442376 | tf_op jit(solution)/shard_map/ppermute | solution.py:190
  32.2 7.4 %collective-permute-start.3 = (bf16[576,128]{1,0:T(8,128)(2,1)S(1)}, bf16[576,128]{1,0:T(8,128)(2,1)S(1)}, u32[]{:S(2)}, u32[]{:S(2)}) collective-permute-start(bf16[576,128]{1,0:T(8,128)(2,1)S(1)} %get-tuple-element.26), channel_id=1, source_target_pairs={{4,0},{16,4},{12,8},{24,12},{20,16},{32,20},{28,24},{40,28},{36,32... | collective-permute-start | bytes 442376 | tf_op jit(solution)/shard_map/ppermute | solution.py:191

commit v5 on v4

--- a/solution.py
+++ b/solution.py
@@ -10,6 +10,10 @@
 BLOCK = 128
 GROUP = 8
 PART = 4
+TILE = 16
+HEADROOM = 14
+FIRST_PAIRS = [[0, 1], [2, 3]]
+SECOND_PAIRS = [[0, 3], [1, 2]]
 LANES = 128
 OWN_FLOPS = 1 * 10 ** 9
 
@@ -169,6 +173,27 @@
 def from_partner(x, n, shard):
     both = lax.all_gather(x, "ctx", axis_index_groups=[[i, i + 1] for i in range(0, n, 2)])
     return jnp.where(shard % 2 == 0, both[1], both[0])
+
+
+def coded(x):
+    largest = jnp.max(jnp.abs(x), axis=0, keepdims=True)
+    power = jnp.ceil(jnp.log2(jnp.maximum(largest, 2.0 ** -100))) - HEADROOM
+    values = (x * jnp.exp2(-power)).astype(jnp.float16)
+    return jnp.concatenate([values, jnp.broadcast_to(power.astype(jnp.float16), (TILE,) + x.shape[1:])], axis=0)
+
+
+def decoded(x):
+    power = x[..., -TILE:-TILE + 1, :].astype(jnp.float32)
+    return x[..., :-TILE, :].astype(jnp.float32) * jnp.exp2(power)
+
+
+def coded_sum(x, pairs):
+    return jnp.sum(decoded(lax.all_gather(coded(x), "head", axis_index_groups=pairs)), axis=0)
+
+
+def plain_sum(x, pairs):
+    both = lax.all_gather(x.astype(jnp.bfloat16), "head", axis_index_groups=pairs)
+    return jnp.sum(both.astype(jnp.float32), axis=0)
 
 
 def shards(queries, latent, out_grad, doc_blocks):
@@ -191,10 +216,8 @@
     skip = lax.ppermute(skip, "ctx", turned(skip_pairs(n)))
     near = near + step.astype(jnp.float32)
     near, skip = lax.optimization_barrier((near, skip))
-    low = (near + skip.astype(jnp.float32)).astype(jnp.bfloat16)
-    low = jnp.sum(lax.all_gather(low, "head", axis_index_groups=[[0, 1], [2, 3]]).astype(jnp.float32), axis=0)
-    parts = lax.all_gather(low.astype(jnp.bfloat16), "head", axis_index_groups=[[0, 3], [1, 2]])
-    return jnp.sum(parts.astype(jnp.float32), axis=0).T
+    low = near + skip.astype(jnp.float32)
+    return plain_sum(coded_sum(low, FIRST_PAIRS), SECOND_PAIRS).T
 
 
 def solution(mesh):

time: 53.5 us -> 53.7 us (level)
  no operation moved by 1% of the time
where the time goes in v5:
time: 53.7 us; the launch traced here: 53.5 us
  blocking collectives  19.3 us (36%)
  starting transfers between devices  17.9 us (33%)
  Pallas kernels  6.19 us (12%)
  waiting for transfers between devices  5.26 us (10%)
  local copies, waits for them, and re-layouts  3.55 us (7%)
  other arithmetic  1.08 us (2%)
    all_gather x1, blocking collectives, plain_sum(): lax.all_gather(x.astype(jnp.bfloat16), 'head', axis_index_groups=pairs)  7.55 us
    ppermute x1, starting transfers between devices, shards(): skip = lax.ppermute(own, 'ctx', skip_pairs(n))  6.65 us
    all_gather x2, blocking collectives, from_partner(): lax.all_gather(x, 'ctx', axis_index_groups=[[i, i + 1] for i in range(0,...  6.41 us
    all_gather x1, blocking collectives, coded_sum(): lax.all_gather(coded(x), 'head', axis_index_groups=pairs)  5.38 us
    ppermute x1, starting transfers between devices, shards(): step = lax.ppermute(step, 'ctx', turned(step_pairs(n)))  4.7 us
    ppermute x1, waiting for transfers between devices, shards(): skip = lax.ppermute(skip, 'ctx', turned(skip_pairs(n)))  4.48 us
    pallas_call x1, Pallas kernels, first_grads(): pl.pallas_call(first_kernel, in_specs=[VMEM] * 8, out_specs=[VMEM] * 4, o...  4.44 us
    ppermute x1, starting transfers between devices, shards(): step = lax.ppermute(own, 'ctx', step_pairs(n))  3.99 us
  transfers between devices with their start and end apart: 4, of which 3 were waited for; matrix products, arithmetic and copies ran while one was open for 7% of the time, Pallas kernels for 3%

profile of v5, /device:TPU:57, one launch (start us, length us, event | category | flops | bytes accessed | tf_op | source)
XLA Modules:
  0.0 53.5 jit_solution(878347078206686408)
XLA Ops:
  0.0 4.0 %collective-permute-start = (bf16[576,128]{1,0:T(8,128)(2,1)}, bf16[576,128]{1,0:T(8,128)(2,1)S(1)}, u32[]{:S(2)}, u32[]{:S(2)}) collective-permute-start(bf16[576,128]{1,0:T(8,128)(2,1)} %bitcast.15), channel_id=1, source_target_pairs={{0,8},{4,12},{8,16},{12,20},{16,24},{20,28},{24,32},{28,36},{32,40... | collective-permute-start | bytes 442376 | tf_op jit(solution)/shard_map/ppermute | solution.py:203
  4.0 6.6 %collective-permute-start.1 = (bf16[576,128]{1,0:T(8,128)(2,1)}, bf16[576,128]{1,0:T(8,128)(2,1)S(1)}, u32[]{:S(2)}, u32[]{:S(2)}) collective-permute-start(bf16[576,128]{1,0:T(8,128)(2,1)} %bitcast.16), channel_id=1, source_target_pairs={{0,4},{4,16},{8,12},{12,24},{16,20},{20,32},{24,28},{28,40},{32,36... | collective-permute-start | bytes 442376 | tf_op jit(solution)/shard_map/ppermute | solution.py:204
  10.7 0.0 copy-start.1
  10.7 0.0 copy-start.2
  10.7 3.5 %copy.6 = bf16[128,16,512]{0,2,1:T(8,128)(2,1)S(1)} copy(bf16[128,16,512]{2,1,0:T(8,128)(2,1)} %param.6) | data formatting | bytes 4194304 | tf_op args[2]
  14.2 0.0 copy-start
  14.2 0.0 copy-done.1
  14.2 0.0 copy-done.2
  14.3 0.5 own_grads.1
  14.7 0.5 collective-permute-done.step_ref
  15.2 4.4 %all-gather = bf16[1152,128]{1,0:T(8,128)(2,1)S(1)} all-gather(bf16[576,128]{1,0:T(8,128)(2,1)S(1)} %collective-permute-done.step_ref), channel_id=2, replica_groups={{0,4},{8,12},{16,20},{24,28},{32,36},{40,44},{48,52},{56,60},{64,68},{7..., dimensions={0}, use_global_device_ids=true | all-gather | bytes 442368 | tf_op jit(solution)/shard_map/all_gather | solution.py:174
  19.6 0.0 copy-done
  19.6 1.3 %products.1 = (f32[256,2048]{1,0:T(8,128)S(1)}, f32[128,2048]{1,0:T(8,128)S(1)}) custom-call(bf16[16,576,128]{2,1,0:T(8,128)(2,1)S(1)} %bitcast.13, bf16[16,512,128]{2,1,0:T(8,128)(2,1)S(1)} %bitcast.11, bf16[576,128]{1,0:T(8,128)(2,1)S(1)} %collective-permute-done.step_ref, bf16[576,128]{1,0:T(8,128)(2,1)S(1)} %bitcast.18), custom_call_target="tpu_custom_call" | custom-call | tf_op jit(solution)/shard_map/products/pallas_call | solution.py:99
  20.9 0.0 collective-permute-done.1.skip_ref
  20.9 4.4 %first_grads.1 = (bf16[576,128]{1,0:T(8,128)(2,1)S(1)}, bf16[576,128]{1,0:T(8,128)(2,1)S(1)}, f32[576,128]{1,0:T(8,128)S(1)}, f32[576,128]{1,0:T(8,128)S(1)}) custom-call(s32[8,128]{1,0:T(8,128)S(1)} %get-tuple-element.17.seen_ref, bf16[16,576,128]{2,1,0:T(8,128)(2,1)S(1)} %bitcast.14, bf16[16,512,128]{2,1,0:T(8,128)(2,1)S(1)} %bitcast.12, ...), custom_call_target="tpu_custom_call" | custom-call | tf_op jit(solution)/shard_map/first_grads/pallas_call | solution.py:161
  25.4 2.0 %all-gather.1 = bf16[1152,128]{1,0:T(8,128)(2,1)S(1)} all-gather(bf16[576,128]{1,0:T(8,128)(2,1)S(1)} %get-tuple-element.24), channel_id=3, replica_groups={{0,4},{8,12},{16,20},{24,28},{32,36},{40,44},{48,52},{56,60},{64,68},{7..., dimensions={0}, use_global_device_ids=true | all-gather | bytes 442368 | tf_op jit(solution)/shard_map/all_gather | solution.py:174
  27.4 0.1 fusion
  27.5 4.7 %collective-permute-start.2 = (bf16[576,128]{1,0:T(8,128)(2,1)S(1)}, bf16[576,128]{1,0:T(8,128)(2,1)S(1)}, u32[]{:S(2)}, u32[]{:S(2)}) collective-permute-start(bf16[576,128]{1,0:T(8,128)(2,1)S(1)} %fusion), channel_id=1, source_target_pairs={{8,0},{12,4},{16,8},{20,12},{24,16},{28,20},{32,24},{36,28},{40,32... | collective-permute-start | bytes 442376 | tf_op jit(solution)/shard_map/ppermute | solution.py:215
  32.2 2.6 %collective-permute-start.3 = (bf16[576,128]{1,0:T(8,128)(2,1)S(1)}, bf16[576,128]{1,0:T(8,128)(2,1)S(1)}, u32[]{:S(2)}, u32[]{:S(2)}) collective-permute-start(bf16[576,128]{1,0:T(8,128)(2,1)S(1)} %get-tuple-element.26), channel_id=1, source_target_pairs={{4,0},{16,4},{12,8},{24,12},{20,16},{32,20},{28,24},{40,28},{36,32... | collective-permute-start | bytes 442376 | tf_op jit(solution)/shard_map/ppermute | solution.py:216
  34.7 0.3 collective-permute-done.2
  35.0 4.5 %collective-permute-done.3 = bf16[576,128]{1,0:T(8,128)(2,1)S(1)} collective-permute-done((bf16[576,128]{1,0:T(8,128)(2,1)S(1)}, bf16[576,128]{1,0:T(8,128)(2,1)S(1)}, u32[]{:S(2)}, u32[]{:S(2)}) %collective-permute-start.3) | collective-permute-done | bytes 147488 | tf_op jit(solution)/shard_map/ppermute | solution.py:216
  39.6 0.1 multiply_convert_fusion
  39.7 5.4 %all-gather.2 = f16[1184,128]{1,0:T(8,128)(2,1)S(1)} all-gather(f16[592,128]{1,0:T(8,128)(2,1)S(1)} %pad_maximum_fusion), channel_id=4, replica_groups={{0,1},{2,3},{4,5},{6,7},{8,9},{10,11},{12,13},{14,15},{16,17},{18,19},{..., dimensions={0}, use_global_device_ids=true | all-gather | bytes 454656 | tf_op jit(solution)/shard_map/all_gather | solution.py:191
  45.1 0.1 multiply_reduce_fusion
  45.2 7.6 %all-gather.3 = bf16[1152,128]{1,0:T(8,128)(2,1)S(1)} all-gather(bf16[576,128]{1,0:T(8,128)(2,1)S(1)} %multiply_reduce_fusion), channel_id=5, replica_groups={{0,3},{1,2},{4,7},{5,6},{8,11},{9,10},{12,15},{13,14},{16,19},{17,18},{..., dimensions={0}, use_global_device_ids=true | all-gather | bytes 442368 | tf_op jit(solution)/shard_map/all_gather | solution.py:195
  52.7 0.8 %convert_reduce_fusion = f32[576,128]{1,0:T(8,128)} fusion(bf16[2,576,128]{2,1,0:T(8,128)(2,1)S(1)} %bitcast.22), kind=kLoop, calls=%fused_computation | loop fusion | flops 221184 | bytes 589824 | tf_op jit(solution)/shard_map/reduce_sum | solution.py:196
  (7 shorter events, 0.2 us)
Async XLA Ops:
  0.0 15.2 %collective-permute-start = (bf16[576,128]{1,0:T(8,128)(2,1)}, bf16[576,128]{1,0:T(8,128)(2,1)S(1)}, u32[]{:S(2)}, u32[]{:S(2)}) collective-permute-start(bf16[576,128]{1,0:T(8,128)(2,1)} %bitcast.15), channel_id=1, source_target_pairs={{0,8},{4,12},{8,16},{12,20},{16,24},{20,28},{24,32},{28,36},{32,40... | collective-permute-start | bytes 442376 | tf_op jit(solution)/shard_map/ppermute | solution.py:203
  4.0 16.9 %collective-permute-start.1 = (bf16[576,128]{1,0:T(8,128)(2,1)}, bf16[576,128]{1,0:T(8,128)(2,1)S(1)}, u32[]{:S(2)}, u32[]{:S(2)}) collective-permute-start(bf16[576,128]{1,0:T(8,128)(2,1)} %bitcast.16), channel_id=1, source_target_pairs={{0,4},{4,16},{8,12},{12,24},{16,20},{20,32},{24,28},{28,40},{32,36... | collective-permute-start | bytes 442376 | tf_op jit(solution)/shard_map/ppermute | solution.py:204
  10.7 3.6 %copy-start.1 = (bf16[128,576]{0,1:T(8,128)(2,1)S(1)}, bf16[128,576]{0,1:T(8,128)(2,1)}, u32[]{:S(2)}) copy-start(bf16[128,576]{0,1:T(8,128)(2,1)} %param.5) | copy-start | bytes 442372
  10.7 3.6 %copy-start.2 = (s32[64]{0:T(128)S(1)}, s32[64]{0:T(128)}, u32[]{:S(2)}) copy-start(s32[64]{0:T(128)} %param.7) | copy-start | bytes 772
  14.2 5.4 %copy-start = (bf16[128,16,576]{0,2,1:T(8,128)(2,1)S(1)}, bf16[128,16,576]{0,2,1:T(8,128)(2,1)}, u32[]{:S(2)}) copy-start(bf16[128,16,576]{0,2,1:T(8,128)(2,1)} %param.4) | copy-start | bytes 7077892
  27.5 7.6 %collective-permute-start.2 = (bf16[576,128]{1,0:T(8,128)(2,1)S(1)}, bf16[576,128]{1,0:T(8,128)(2,1)S(1)}, u32[]{:S(2)}, u32[]{:S(2)}) collective-permute-start(bf16[576,128]{1,0:T(8,128)(2,1)S(1)} %fusion), channel_id=1, source_target_pairs={{8,0},{12,4},{16,8},{20,12},{24,16},{28,20},{32,24},{36,28},{40,32... | collective-permute-start | bytes 442376 | tf_op jit(solution)/shard_map/ppermute | solution.py:215
  32.2 7.4 %collective-permute-start.3 = (bf16[576,128]{1,0:T(8,128)(2,1)S(1)}, bf16[576,128]{1,0:T(8,128)(2,1)S(1)}, u32[]{:S(2)}, u32[]{:S(2)}) collective-permute-start(bf16[576,128]{1,0:T(8,128)(2,1)S(1)} %get-tuple-element.26), channel_id=1, source_target_pairs={{4,0},{16,4},{12,8},{24,12},{20,16},{32,20},{28,24},{40,28},{36,32... | collective-permute-start | bytes 442376 | tf_op jit(solution)/shard_map/ppermute | solution.py:216

commit v6 on v5

--- a/solution.py
+++ b/solution.py
@@ -80,50 +80,26 @@
     )(shard, doc_blocks, g, own)
 
 
-def products_kernel(q_ref, g_ref, step_ref, own_ref, scores_ref, grads_ref):
-    heads, lat, blk = g_ref.shape
-    rows = jnp.concatenate([step_ref[...].T, own_ref[...].T], axis=0)
-    for at in range(0, heads, GROUP):
-        where = slice(at * blk, (at + GROUP) * blk)
-        scores = jnp.dot(rows, side_by_side(q_ref, at, GROUP), preferred_element_type=jnp.float32)
-        key = lax.broadcasted_iota(jnp.int32, scores[blk:].shape, 0)
-        query = lax.broadcasted_iota(jnp.int32, scores[blk:].shape, 1) & (blk - 1)
-        scores_ref[:blk, where] = scores[:blk]
-        scores_ref[blk:, where] = jnp.where(key <= query, scores[blk:], -jnp.inf)
-        grads_ref[:, where] = jnp.dot(
-            rows[:blk, :lat], side_by_side(g_ref, at, GROUP), preferred_element_type=jnp.float32)
-
-
-def products(q, g, step, own):
-    heads, width, rows = q.shape
-    return pl.pallas_call(
-        products_kernel,
-        in_specs=[VMEM] * 4, out_specs=[VMEM, VMEM],
-        out_shape=[
-            jax.ShapeDtypeStruct((2 * rows, heads * rows), jnp.float32),
-            jax.ShapeDtypeStruct((rows, heads * rows), jnp.float32),
-        ],
-        compiler_params=pltpu.CompilerParams(vmem_limit_bytes=30 * 1024 * 1024),
-        name="products",
-    )(q, g, step, own)
-
-
-def first_kernel(seen_ref, q_ref, g_ref, swap_ref, skip_ref, near_s, step_g, own_g,
+def first_kernel(seen_ref, q_ref, g_ref, swap_ref, skip_ref, step_ref, own_ref, own_g,
                  swap_out, skip_out, step_out, own_out):
     heads, lat, blk = g_ref.shape
-    rows = jnp.concatenate([swap_ref[...].T, skip_ref[...].T], axis=0)
+    rows = jnp.concatenate([ref[...].T for ref in (swap_ref, skip_ref, step_ref, own_ref)], axis=0)
+    cols = PART * blk
+    late = (lax.broadcasted_iota(jnp.int32, (blk, cols), 0)
+            > (lax.broadcasted_iota(jnp.int32, (blk, cols), 1) & (blk - 1)))
 
     def products_of(at):
         q = side_by_side(q_ref, at, PART)
         g = side_by_side(g_ref, at, PART)
         scores = jnp.dot(rows, q, preferred_element_type=jnp.float32)
-        grad_probs = jnp.dot(rows[:, :lat], g, preferred_element_type=jnp.float32)
+        grad_probs = jnp.dot(rows[:3 * blk, :lat], g, preferred_element_type=jnp.float32)
         return at, q, g, scores, grad_probs
 
     def sums_of(at, q, g, scores, grad_probs):
         where = slice(at * blk, (at + PART) * blk)
-        grad_probs = jnp.concatenate([grad_probs, step_g[:, where], own_g[:, where]], axis=0)
-        parts = [scores[:blk], scores[blk:], near_s[:blk, where], near_s[blk:, where]]
+        grad_probs = jnp.concatenate([grad_probs, own_g[:, where]], axis=0)
+        parts = [scores[j * blk:(j + 1) * blk] for j in range(4)]
+        parts[3] = jnp.where(late, -jnp.inf, parts[3])
         tops = [jnp.max(part, axis=0, keepdims=True) for part in parts]
         top = tops[3]
         for j in range(3):
@@ -154,7 +130,7 @@
         ref[lat:, :] = key[lat:, mine].astype(ref.dtype)
 
 
-def first_grads(seen, q, g, swap, skip, near_scores, step_grads, own_grads):
+def first_grads(seen, q, g, swap, skip, step, own, own_grads):
     heads, width, rows = q.shape
     sent = jax.ShapeDtypeStruct((width, rows), jnp.bfloat16)
     kept = jax.ShapeDtypeStruct((width, rows), jnp.float32)
@@ -163,7 +139,7 @@
         in_specs=[VMEM] * 8, out_specs=[VMEM] * 4, out_shape=[sent, sent, kept, kept],
         compiler_params=pltpu.CompilerParams(vmem_limit_bytes=30 * 1024 * 1024),
         name="first_grads",
-    )(seen, q, g, swap, skip, near_scores, step_grads, own_grads)
+    )(seen, q, g, swap, skip, step, own, own_grads)
 
 
 def after(x, *others):
@@ -207,8 +183,7 @@
     seen, of_own = own_grads(shard.reshape(1), doc_blocks.reshape(1, -1), g, own)
     step = after(step, of_own)
     swap = from_partner(step, n, shard)
-    near_scores, of_step = products(q, g, step, own)
-    swap, skip, step, near = first_grads(seen, q, g, swap, skip, near_scores, of_step, of_own)
+    swap, skip, step, near = first_grads(seen, q, g, swap, skip, step, own, of_own)
     swap = from_partner(swap, n, shard)
     step = (step + swap.astype(jnp.float32)).astype(jnp.bfloat16)
     skip = after(skip, step)

time: 53.7 us -> 53.2 us (level)
    pallas_call x1 -> x0, Pallas kernels: 1.28 us -> none  [products(): pl.pallas_call(products_kernel, in_specs=[VMEM] * 4, out_specs=[VMEM, VME...]
    pallas_call x1, Pallas kernels: 4.44 us -> 5.43 us  [first_grads(): pl.pallas_call(first_kernel, in_specs=[VMEM] * 8, out_specs=[VMEM] * 4, o...]
  transfers between devices with their start and end apart: 4 -> 4, of which waited for: 3 -> 3; matrix products, arithmetic and copies ran while one was open for 7% -> 7% of each run, Pallas kernels for 3% -> 1%
where the time goes in v6:
time: 53.2 us; the launch traced here: 53 us
  blocking collectives  19.1 us (36%)
  starting transfers between devices  17.9 us (34%)
  Pallas kernels  5.9 us (11%)
  waiting for transfers between devices  5.25 us (10%)
  local copies, waits for them, and re-layouts  3.55 us (7%)
  other arithmetic  1.09 us (2%)
    all_gather x1, blocking collectives, plain_sum(): lax.all_gather(x.astype(jnp.bfloat16), 'head', axis_index_groups=pairs)  7.59 us
    ppermute x1, starting transfers between devices, shards(): skip = lax.ppermute(own, 'ctx', skip_pairs(n))  6.65 us
    all_gather x2, blocking collectives, from_partner(): lax.all_gather(x, 'ctx', axis_index_groups=[[i, i + 1] for i in range(0,...  6.41 us
    pallas_call x1, Pallas kernels, first_grads(): pl.pallas_call(first_kernel, in_specs=[VMEM] * 8, out_specs=[VMEM] * 4, o...  5.43 us
    all_gather x1, blocking collectives, coded_sum(): lax.all_gather(coded(x), 'head', axis_index_groups=pairs)  5.14 us
    ppermute x1, starting transfers between devices, shards(): step = lax.ppermute(step, 'ctx', turned(step_pairs(n)))  4.7 us
    ppermute x1, waiting for transfers between devices, shards(): skip = lax.ppermute(skip, 'ctx', turned(skip_pairs(n)))  4.48 us
    ppermute x1, starting transfers between devices, shards(): step = lax.ppermute(own, 'ctx', step_pairs(n))  3.99 us
  transfers between devices with their start and end apart: 4, of which 3 were waited for; matrix products, arithmetic and copies ran while one was open for 7% of the time, Pallas kernels for 1%

profile of v6, /device:TPU:57, one launch (start us, length us, event | category | flops | bytes accessed | tf_op | source)
XLA Modules:
  0.0 53.0 jit_solution(6694485561351945473)
XLA Ops:
  0.0 4.0 %collective-permute-start = (bf16[576,128]{1,0:T(8,128)(2,1)}, bf16[576,128]{1,0:T(8,128)(2,1)S(1)}, u32[]{:S(2)}, u32[]{:S(2)}) collective-permute-start(bf16[576,128]{1,0:T(8,128)(2,1)} %bitcast.13), channel_id=1, source_target_pairs={{0,8},{4,12},{8,16},{12,20},{16,24},{20,28},{24,32},{28,36},{32,40... | collective-permute-start | bytes 442376 | tf_op jit(solution)/shard_map/ppermute | solution.py:179
  4.0 6.6 %collective-permute-start.1 = (bf16[576,128]{1,0:T(8,128)(2,1)}, bf16[576,128]{1,0:T(8,128)(2,1)S(1)}, u32[]{:S(2)}, u32[]{:S(2)}) collective-permute-start(bf16[576,128]{1,0:T(8,128)(2,1)} %bitcast.14), channel_id=1, source_target_pairs={{0,4},{4,16},{8,12},{12,24},{16,20},{20,32},{24,28},{28,40},{32,36... | collective-permute-start | bytes 442376 | tf_op jit(solution)/shard_map/ppermute | solution.py:180
  10.7 0.0 copy-start.1
  10.7 0.0 copy-start.2
  10.7 3.5 %copy.6 = bf16[128,16,512]{0,2,1:T(8,128)(2,1)S(1)} copy(bf16[128,16,512]{2,1,0:T(8,128)(2,1)} %param.6) | data formatting | bytes 4194304 | tf_op args[2]
  14.2 0.0 copy-done.1
  14.2 0.0 copy-done.2
  14.2 0.0 copy-start
  14.3 0.5 own_grads.1
  14.7 0.5 collective-permute-done.step_ref
  15.2 4.4 %all-gather = bf16[1152,128]{1,0:T(8,128)(2,1)S(1)} all-gather(bf16[576,128]{1,0:T(8,128)(2,1)S(1)} %collective-permute-done.step_ref), channel_id=2, replica_groups={{0,4},{8,12},{16,20},{24,28},{32,36},{40,44},{48,52},{56,60},{64,68},{7..., dimensions={0}, use_global_device_ids=true | all-gather | bytes 442368 | tf_op jit(solution)/shard_map/all_gather | solution.py:150
  19.6 0.0 collective-permute-done.1.skip_ref
  19.6 0.0 copy-done
  19.6 5.4 %first_grads.1 = (bf16[576,128]{1,0:T(8,128)(2,1)S(1)}, bf16[576,128]{1,0:T(8,128)(2,1)S(1)}, f32[576,128]{1,0:T(8,128)S(1)}, f32[576,128]{1,0:T(8,128)S(1)}) custom-call(s32[8,128]{1,0:T(8,128)S(1)} %get-tuple-element.15.seen_ref, bf16[16,576,128]{2,1,0:T(8,128)(2,1)S(1)} %bitcast.12, bf16[16,512,128]{2,1,0:T(8,128)(2,1)S(1)} %bitcast.11, ...), custom_call_target="tpu_custom_call" | custom-call | tf_op jit(solution)/shard_map/first_grads/pallas_call | solution.py:137
  25.1 2.0 %all-gather.1 = bf16[1152,128]{1,0:T(8,128)(2,1)S(1)} all-gather(bf16[576,128]{1,0:T(8,128)(2,1)S(1)} %get-tuple-element.20), channel_id=3, replica_groups={{0,4},{8,12},{16,20},{24,28},{32,36},{40,44},{48,52},{56,60},{64,68},{7..., dimensions={0}, use_global_device_ids=true | all-gather | bytes 442368 | tf_op jit(solution)/shard_map/all_gather | solution.py:150
  27.1 0.1 fusion
  27.2 4.7 %collective-permute-start.2 = (bf16[576,128]{1,0:T(8,128)(2,1)S(1)}, bf16[576,128]{1,0:T(8,128)(2,1)S(1)}, u32[]{:S(2)}, u32[]{:S(2)}) collective-permute-start(bf16[576,128]{1,0:T(8,128)(2,1)S(1)} %fusion), channel_id=1, source_target_pairs={{8,0},{12,4},{16,8},{20,12},{24,16},{28,20},{32,24},{36,28},{40,32... | collective-permute-start | bytes 442376 | tf_op jit(solution)/shard_map/ppermute | solution.py:190
  31.9 2.6 %collective-permute-start.3 = (bf16[576,128]{1,0:T(8,128)(2,1)S(1)}, bf16[576,128]{1,0:T(8,128)(2,1)S(1)}, u32[]{:S(2)}, u32[]{:S(2)}) collective-permute-start(bf16[576,128]{1,0:T(8,128)(2,1)S(1)} %get-tuple-element.22), channel_id=1, source_target_pairs={{4,0},{16,4},{12,8},{24,12},{20,16},{32,20},{28,24},{40,28},{36,32... | collective-permute-start | bytes 442376 | tf_op jit(solution)/shard_map/ppermute | solution.py:191
  34.4 0.3 collective-permute-done.2
  34.8 4.5 %collective-permute-done.3 = bf16[576,128]{1,0:T(8,128)(2,1)S(1)} collective-permute-done((bf16[576,128]{1,0:T(8,128)(2,1)S(1)}, bf16[576,128]{1,0:T(8,128)(2,1)S(1)}, u32[]{:S(2)}, u32[]{:S(2)}) %collective-permute-start.3) | collective-permute-done | bytes 147488 | tf_op jit(solution)/shard_map/ppermute | solution.py:191
  39.3 0.1 multiply_convert_fusion
  39.4 5.1 %all-gather.2 = f16[1184,128]{1,0:T(8,128)(2,1)S(1)} all-gather(f16[592,128]{1,0:T(8,128)(2,1)S(1)} %pad_maximum_fusion), channel_id=4, replica_groups={{0,1},{2,3},{4,5},{6,7},{8,9},{10,11},{12,13},{14,15},{16,17},{18,19},{..., dimensions={0}, use_global_device_ids=true | all-gather | bytes 454656 | tf_op jit(solution)/shard_map/all_gather | solution.py:167
  44.6 0.1 multiply_reduce_fusion
  44.6 7.6 %all-gather.3 = bf16[1152,128]{1,0:T(8,128)(2,1)S(1)} all-gather(bf16[576,128]{1,0:T(8,128)(2,1)S(1)} %multiply_reduce_fusion), channel_id=5, replica_groups={{0,3},{1,2},{4,7},{5,6},{8,11},{9,10},{12,15},{13,14},{16,19},{17,18},{..., dimensions={0}, use_global_device_ids=true | all-gather | bytes 442368 | tf_op jit(solution)/shard_map/all_gather | solution.py:171
  52.2 0.8 %convert_reduce_fusion = f32[576,128]{1,0:T(8,128)} fusion(bf16[2,576,128]{2,1,0:T(8,128)(2,1)S(1)} %bitcast.20), kind=kLoop, calls=%fused_computation | loop fusion | flops 221184 | bytes 589824 | tf_op jit(solution)/shard_map/reduce_sum | solution.py:172
  (7 shorter events, 0.2 us)
Async XLA Ops:
  0.0 15.2 %collective-permute-start = (bf16[576,128]{1,0:T(8,128)(2,1)}, bf16[576,128]{1,0:T(8,128)(2,1)S(1)}, u32[]{:S(2)}, u32[]{:S(2)}) collective-permute-start(bf16[576,128]{1,0:T(8,128)(2,1)} %bitcast.13), channel_id=1, source_target_pairs={{0,8},{4,12},{8,16},{12,20},{16,24},{20,28},{24,32},{28,36},{32,40... | collective-permute-start | bytes 442376 | tf_op jit(solution)/shard_map/ppermute | solution.py:179
  4.0 15.6 %collective-permute-start.1 = (bf16[576,128]{1,0:T(8,128)(2,1)}, bf16[576,128]{1,0:T(8,128)(2,1)S(1)}, u32[]{:S(2)}, u32[]{:S(2)}) collective-permute-start(bf16[576,128]{1,0:T(8,128)(2,1)} %bitcast.14), channel_id=1, source_target_pairs={{0,4},{4,16},{8,12},{12,24},{16,20},{20,32},{24,28},{28,40},{32,36... | collective-permute-start | bytes 442376 | tf_op jit(solution)/shard_map/ppermute | solution.py:180
  10.7 3.6 %copy-start.1 = (bf16[128,576]{0,1:T(8,128)(2,1)S(1)}, bf16[128,576]{0,1:T(8,128)(2,1)}, u32[]{:S(2)}) copy-start(bf16[128,576]{0,1:T(8,128)(2,1)} %param.5) | copy-start | bytes 442372
  10.7 3.6 %copy-start.2 = (s32[64]{0:T(128)S(1)}, s32[64]{0:T(128)}, u32[]{:S(2)}) copy-start(s32[64]{0:T(128)} %param.7) | copy-start | bytes 772
  14.2 5.4 %copy-start = (bf16[128,16,576]{0,2,1:T(8,128)(2,1)S(1)}, bf16[128,16,576]{0,2,1:T(8,128)(2,1)}, u32[]{:S(2)}) copy-start(bf16[128,16,576]{0,2,1:T(8,128)(2,1)} %param.4) | copy-start | bytes 7077892
  27.2 7.6 %collective-permute-start.2 = (bf16[576,128]{1,0:T(8,128)(2,1)S(1)}, bf16[576,128]{1,0:T(8,128)(2,1)S(1)}, u32[]{:S(2)}, u32[]{:S(2)}) collective-permute-start(bf16[576,128]{1,0:T(8,128)(2,1)S(1)} %fusion), channel_id=1, source_target_pairs={{8,0},{12,4},{16,8},{20,12},{24,16},{28,20},{32,24},{36,28},{40,32... | collective-permute-start | bytes 442376 | tf_op jit(solution)/shard_map/ppermute | solution.py:190
  31.9 7.4 %collective-permute-start.3 = (bf16[576,128]{1,0:T(8,128)(2,1)S(1)}, bf16[576,128]{1,0:T(8,128)(2,1)S(1)}, u32[]{:S(2)}, u32[]{:S(2)}) collective-permute-start(bf16[576,128]{1,0:T(8,128)(2,1)S(1)} %get-tuple-element.22), channel_id=1, source_target_pairs={{4,0},{16,4},{12,8},{24,12},{20,16},{32,20},{28,24},{40,28},{36,32... | collective-permute-start | bytes 442376 | tf_op jit(solution)/shard_map/ppermute | solution.py:191

commit v7 on v6

--- a/solution.py
+++ b/solution.py
@@ -111,9 +111,10 @@
         dot = jnp.sum(raised * grad_probs, axis=0, keepdims=True) * inverse
         low = (raised * inverse).astype(jnp.bfloat16)
         grad_scores = ((raised * (inverse * softmax_scale)) * (grad_probs - dot)).astype(jnp.bfloat16)
-        value = lax.dot_general(g, low, NT, preferred_element_type=jnp.float32)
-        key = lax.dot_general(q, grad_scores, NT, preferred_element_type=jnp.float32)
-        return value, key
+        halves = [slice(0, 2 * blk), slice(2 * blk, 4 * blk)]
+        value = [lax.dot_general(g, low[half], NT, preferred_element_type=jnp.float32) for half in halves]
+        key = [lax.dot_general(q, grad_scores[half], NT, preferred_element_type=jnp.float32) for half in halves]
+        return jnp.concatenate(value, axis=1), jnp.concatenate(key, axis=1)
 
     value = key = None
     after_this = products_of(0)

time: 53.2 us -> 53 us (level)
  no operation moved by 1% of the time
where the time goes in v7:
time: 53 us; the launch traced here: 52.8 us
  blocking collectives  18.9 us (36%)
  starting transfers between devices  17.9 us (34%)
  Pallas kernels  5.97 us (11%)
  waiting for transfers between devices  5.25 us (10%)
  local copies, waits for them, and re-layouts  3.55 us (7%)
  other arithmetic  1.09 us (2%)
    all_gather x1, blocking collectives, plain_sum(): lax.all_gather(x.astype(jnp.bfloat16), 'head', axis_index_groups=pairs)  7.41 us
    ppermute x1, starting transfers between devices, shards(): skip = lax.ppermute(own, 'ctx', skip_pairs(n))  6.65 us
    all_gather x2, blocking collectives, from_partner(): lax.all_gather(x, 'ctx', axis_index_groups=[[i, i + 1] for i in range(0,...  6.41 us
    pallas_call x1, Pallas kernels, first_grads(): pl.pallas_call(first_kernel, in_specs=[VMEM] * 8, out_specs=[VMEM] * 4, o...  5.5 us
    all_gather x1, blocking collectives, coded_sum(): lax.all_gather(coded(x), 'head', axis_index_groups=pairs)  5.06 us
    ppermute x1, starting transfers between devices, shards(): step = lax.ppermute(step, 'ctx', turned(step_pairs(n)))  4.7 us
    ppermute x1, waiting for transfers between devices, shards(): skip = lax.ppermute(skip, 'ctx', turned(skip_pairs(n)))  4.47 us
    ppermute x1, starting transfers between devices, shards(): step = lax.ppermute(own, 'ctx', step_pairs(n))  3.99 us
  transfers between devices with their start and end apart: 4, of which 3 were waited for; matrix products, arithmetic and copies ran while one was open for 7% of the time, Pallas kernels for 1%

profile of v7, /device:TPU:57, one launch (start us, length us, event | category | flops | bytes accessed | tf_op | source)
XLA Modules:
  0.0 52.8 jit_solution(11334261171278440517)
XLA Ops:
  0.0 4.0 %collective-permute-start = (bf16[576,128]{1,0:T(8,128)(2,1)}, bf16[576,128]{1,0:T(8,128)(2,1)S(1)}, u32[]{:S(2)}, u32[]{:S(2)}) collective-permute-start(bf16[576,128]{1,0:T(8,128)(2,1)} %bitcast.13), channel_id=1, source_target_pairs={{0,8},{4,12},{8,16},{12,20},{16,24},{20,28},{24,32},{28,36},{32,40... | collective-permute-start | bytes 442376 | tf_op jit(solution)/shard_map/ppermute | solution.py:180
  4.0 6.6 %collective-permute-start.1 = (bf16[576,128]{1,0:T(8,128)(2,1)}, bf16[576,128]{1,0:T(8,128)(2,1)S(1)}, u32[]{:S(2)}, u32[]{:S(2)}) collective-permute-start(bf16[576,128]{1,0:T(8,128)(2,1)} %bitcast.14), channel_id=1, source_target_pairs={{0,4},{4,16},{8,12},{12,24},{16,20},{20,32},{24,28},{28,40},{32,36... | collective-permute-start | bytes 442376 | tf_op jit(solution)/shard_map/ppermute | solution.py:181
  10.7 0.0 copy-start.1
  10.7 0.0 copy-start.2
  10.7 3.5 %copy.6 = bf16[128,16,512]{0,2,1:T(8,128)(2,1)S(1)} copy(bf16[128,16,512]{2,1,0:T(8,128)(2,1)} %param.6) | data formatting | bytes 4194304 | tf_op args[2]
  14.2 0.0 copy-done.1
  14.2 0.0 copy-done.2
  14.2 0.0 copy-start
  14.3 0.5 own_grads.1
  14.7 0.5 collective-permute-done.step_ref
  15.2 4.4 %all-gather = bf16[1152,128]{1,0:T(8,128)(2,1)S(1)} all-gather(bf16[576,128]{1,0:T(8,128)(2,1)S(1)} %collective-permute-done.step_ref), channel_id=2, replica_groups={{0,4},{8,12},{16,20},{24,28},{32,36},{40,44},{48,52},{56,60},{64,68},{7..., dimensions={0}, use_global_device_ids=true | all-gather | bytes 442368 | tf_op jit(solution)/shard_map/all_gather | solution.py:151
  19.6 0.0 collective-permute-done.1.skip_ref
  19.6 0.0 copy-done
  19.6 5.5 %first_grads.1 = (bf16[576,128]{1,0:T(8,128)(2,1)S(1)}, bf16[576,128]{1,0:T(8,128)(2,1)S(1)}, f32[576,128]{1,0:T(8,128)S(1)}, f32[576,128]{1,0:T(8,128)S(1)}) custom-call(s32[8,128]{1,0:T(8,128)S(1)} %get-tuple-element.15.seen_ref, bf16[16,576,128]{2,1,0:T(8,128)(2,1)S(1)} %bitcast.12, bf16[16,512,128]{2,1,0:T(8,128)(2,1)S(1)} %bitcast.11, ...), custom_call_target="tpu_custom_call" | custom-call | tf_op jit(solution)/shard_map/first_grads/pallas_call | solution.py:138
  25.2 2.0 %all-gather.1 = bf16[1152,128]{1,0:T(8,128)(2,1)S(1)} all-gather(bf16[576,128]{1,0:T(8,128)(2,1)S(1)} %get-tuple-element.20), channel_id=3, replica_groups={{0,4},{8,12},{16,20},{24,28},{32,36},{40,44},{48,52},{56,60},{64,68},{7..., dimensions={0}, use_global_device_ids=true | all-gather | bytes 442368 | tf_op jit(solution)/shard_map/all_gather | solution.py:151
  27.2 0.1 fusion
  27.2 4.7 %collective-permute-start.2 = (bf16[576,128]{1,0:T(8,128)(2,1)S(1)}, bf16[576,128]{1,0:T(8,128)(2,1)S(1)}, u32[]{:S(2)}, u32[]{:S(2)}) collective-permute-start(bf16[576,128]{1,0:T(8,128)(2,1)S(1)} %fusion), channel_id=1, source_target_pairs={{8,0},{12,4},{16,8},{20,12},{24,16},{28,20},{32,24},{36,28},{40,32... | collective-permute-start | bytes 442376 | tf_op jit(solution)/shard_map/ppermute | solution.py:191
  31.9 2.6 %collective-permute-start.3 = (bf16[576,128]{1,0:T(8,128)(2,1)S(1)}, bf16[576,128]{1,0:T(8,128)(2,1)S(1)}, u32[]{:S(2)}, u32[]{:S(2)}) collective-permute-start(bf16[576,128]{1,0:T(8,128)(2,1)S(1)} %get-tuple-element.22), channel_id=1, source_target_pairs={{4,0},{16,4},{12,8},{24,12},{20,16},{32,20},{28,24},{40,28},{36,32... | collective-permute-start | bytes 442376 | tf_op jit(solution)/shard_map/ppermute | solution.py:192
  34.5 0.3 collective-permute-done.2
  34.8 4.5 %collective-permute-done.3 = bf16[576,128]{1,0:T(8,128)(2,1)S(1)} collective-permute-done((bf16[576,128]{1,0:T(8,128)(2,1)S(1)}, bf16[576,128]{1,0:T(8,128)(2,1)S(1)}, u32[]{:S(2)}, u32[]{:S(2)}) %collective-permute-start.3) | collective-permute-done | bytes 147488 | tf_op jit(solution)/shard_map/ppermute | solution.py:192
  39.4 0.1 multiply_convert_fusion
  39.5 5.1 %all-gather.2 = f16[1184,128]{1,0:T(8,128)(2,1)S(1)} all-gather(f16[592,128]{1,0:T(8,128)(2,1)S(1)} %pad_maximum_fusion), channel_id=4, replica_groups={{0,1},{2,3},{4,5},{6,7},{8,9},{10,11},{12,13},{14,15},{16,17},{18,19},{..., dimensions={0}, use_global_device_ids=true | all-gather | bytes 454656 | tf_op jit(solution)/shard_map/all_gather | solution.py:168
  44.6 0.1 multiply_reduce_fusion
  44.6 7.4 %all-gather.3 = bf16[1152,128]{1,0:T(8,128)(2,1)S(1)} all-gather(bf16[576,128]{1,0:T(8,128)(2,1)S(1)} %multiply_reduce_fusion), channel_id=5, replica_groups={{0,3},{1,2},{4,7},{5,6},{8,11},{9,10},{12,15},{13,14},{16,19},{17,18},{..., dimensions={0}, use_global_device_ids=true | all-gather | bytes 442368 | tf_op jit(solution)/shard_map/all_gather | solution.py:172
  52.0 0.8 %convert_reduce_fusion = f32[576,128]{1,0:T(8,128)} fusion(bf16[2,576,128]{2,1,0:T(8,128)(2,1)S(1)} %bitcast.20), kind=kLoop, calls=%fused_computation | loop fusion | flops 221184 | bytes 589824 | tf_op jit(solution)/shard_map/reduce_sum | solution.py:173
  (7 shorter events, 0.2 us)
Async XLA Ops:
  0.0 15.2 %collective-permute-start = (bf16[576,128]{1,0:T(8,128)(2,1)}, bf16[576,128]{1,0:T(8,128)(2,1)S(1)}, u32[]{:S(2)}, u32[]{:S(2)}) collective-permute-start(bf16[576,128]{1,0:T(8,128)(2,1)} %bitcast.13), channel_id=1, source_target_pairs={{0,8},{4,12},{8,16},{12,20},{16,24},{20,28},{24,32},{28,36},{32,40... | collective-permute-start | bytes 442376 | tf_op jit(solution)/shard_map/ppermute | solution.py:180
  4.0 15.6 %collective-permute-start.1 = (bf16[576,128]{1,0:T(8,128)(2,1)}, bf16[576,128]{1,0:T(8,128)(2,1)S(1)}, u32[]{:S(2)}, u32[]{:S(2)}) collective-permute-start(bf16[576,128]{1,0:T(8,128)(2,1)} %bitcast.14), channel_id=1, source_target_pairs={{0,4},{4,16},{8,12},{12,24},{16,20},{20,32},{24,28},{28,40},{32,36... | collective-permute-start | bytes 442376 | tf_op jit(solution)/shard_map/ppermute | solution.py:181
  10.7 3.6 %copy-start.1 = (bf16[128,576]{0,1:T(8,128)(2,1)S(1)}, bf16[128,576]{0,1:T(8,128)(2,1)}, u32[]{:S(2)}) copy-start(bf16[128,576]{0,1:T(8,128)(2,1)} %param.5) | copy-start | bytes 442372
  10.7 3.6 %copy-start.2 = (s32[64]{0:T(128)S(1)}, s32[64]{0:T(128)}, u32[]{:S(2)}) copy-start(s32[64]{0:T(128)} %param.7) | copy-start | bytes 772
  14.2 5.4 %copy-start = (bf16[128,16,576]{0,2,1:T(8,128)(2,1)S(1)}, bf16[128,16,576]{0,2,1:T(8,128)(2,1)}, u32[]{:S(2)}) copy-start(bf16[128,16,576]{0,2,1:T(8,128)(2,1)} %param.4) | copy-start | bytes 7077892
  27.2 7.6 %collective-permute-start.2 = (bf16[576,128]{1,0:T(8,128)(2,1)S(1)}, bf16[576,128]{1,0:T(8,128)(2,1)S(1)}, u32[]{:S(2)}, u32[]{:S(2)}) collective-permute-start(bf16[576,128]{1,0:T(8,128)(2,1)S(1)} %fusion), channel_id=1, source_target_pairs={{8,0},{12,4},{16,8},{20,12},{24,16},{28,20},{32,24},{36,28},{40,32... | collective-permute-start | bytes 442376 | tf_op jit(solution)/shard_map/ppermute | solution.py:191
  31.9 7.4 %collective-permute-start.3 = (bf16[576,128]{1,0:T(8,128)(2,1)S(1)}, bf16[576,128]{1,0:T(8,128)(2,1)S(1)}, u32[]{:S(2)}, u32[]{:S(2)}) collective-permute-start(bf16[576,128]{1,0:T(8,128)(2,1)S(1)} %get-tuple-element.22), channel_id=1, source_target_pairs={{4,0},{16,4},{12,8},{24,12},{20,16},{32,20},{28,24},{40,28},{36,32... | collective-permute-start | bytes 442376 | tf_op jit(solution)/shard_map/ppermute | solution.py:192
